TPU v7x, 32 devices: a whole 2x2x4 slice. The times are simulated.
32 devices in a mesh: group: 4 (over x, core), fsdp: 8 (over z, y).
Axes of the slice: x: 2, y: 2, z: 4, core: 2. Of those that a mesh axis runs over, the one named last changes fastest.
Arguments:
- hidden: bfloat16 [32, 128, 8192], P('group', None, 'fsdp'), may hold values from -6 to 6
- norm_gain: bfloat16 [8192], replicated, may hold values from 0.099609375 to 1.8984375
- w_query: bfloat16 [8192, 8192], P('group', 'fsdp'), may hold values from -0.0625 to 0.0625
- key_projection_weight: bfloat16 [8192, 1024], P('group'), may hold values from -0.0625 to 0.0625
- value_projection_weight: bfloat16 [8192, 1024], P('group'), may hold values from -0.0625 to 0.0625
- prompt_key_cache: bfloat16 [2048, 1024], P('group'), may hold values from -74 to 74
- prompt_value_cache: bfloat16 [2048, 1024], P('group'), may hold values from -6 to 6
- keep_flag: int32 [32], replicated, may hold values from 0 to 1, as said below
- destination: int32 [32], replicated, may hold values from 0 to 15, as said below
- row_counts: int32 [32], replicated, may hold values from 32 to 128
Outputs:
- attended: bfloat16 [16, 128, 8192], P('group', None, 'fsdp')
Inputs may be any that keep to these rules, and one draw needn't show every extreme that they name: `keep_flag`: exactly 16 blocks are kept. `destination`: the kept blocks name the slots 0 to 15, each exactly once. Among the 8 blocks g * 8 to g * 8 + 7, the kept ones that name a slot of d * 4 to d * 4 + 3 number either 0 or exactly 1. Entries of dropped blocks are arbitrary slot numbers.
All inputs are finite; a program needn't handle non-finite values.
Results may differ from a plain program's by a relative error of at most 0.012.
The roundings to bfloat16 on the way count: a program that leaves them out, or rounds other values in their place, can miss the bound.
Values may be sent and summed in bfloat16 or wider, within the bound.
A program may use at most 192 MiB of HBM per device.

v0:
```python
import jax
import jax.numpy as jnp
from jax import lax
from jax.sharding import PartitionSpec as P

QUERY_HEADS = 64
KEY_VALUE_HEADS = 8
HEAD_SIZE = 128
PROMPT_TOKENS = 2048
IN_DEV = 8
CAP = 1
OUT_DEV = 4


EPSILON = 1e-05
ROPE_THETA = 500000.0
CONTEXT_BASE = 8192.0
STRETCH = 8.0
MASKED_SCORE = -1e30


def rope_tables(length, offset):
    half_dim = HEAD_SIZE // 2
    base_rate = ROPE_THETA ** (-(jnp.arange(half_dim, dtype=jnp.float32) * 2.0 / HEAD_SIZE))
    ratio = CONTEXT_BASE * base_rate / (2.0 * jnp.pi)
    smooth = jnp.clip((ratio - 1.0) / 3.0, 0.0, 1.0)
    inverse_rate = (1.0 - smooth) * base_rate / STRETCH + smooth * base_rate
    token_positions = jnp.arange(length, dtype=jnp.float32) + offset
    angles = token_positions[:, None] * inverse_rate[None, :]
    return (jnp.cos(angles), jnp.sin(angles))


def rotate(values, cosine, sine_table):
    half_dim = values.shape[-1] // 2
    first_half = values[..., :half_dim]
    second = values[..., half_dim:]
    cosine = cosine[:, None, :]
    sine_table = sine_table[:, None, :]
    return jnp.concatenate(
        [first_half * cosine - second * sine_table, second * cosine + first_half * sine_table],
        axis=-1,
    )


def routing(keep_flag, destination):
    block_total = keep_flag.shape[0]
    block_index = jnp.arange(block_total, dtype=jnp.int32)
    block_owner = block_index // IN_DEV
    is_live = keep_flag == 1
    target = destination // OUT_DEV
    earlier = (
        (block_owner[:, None] == block_owner[None, :])
        & (target[:, None] == target[None, :])
        & is_live[None, :]
        & (block_index[None, :] < block_index[:, None])
    )
    order_rank = jnp.sum(earlier.astype(jnp.int32), axis=1)
    return (block_owner, is_live, target, order_rank)


def pack_for_send(values, keep_flag, destination):
    group_count = lax.axis_size("group")
    my_group = lax.axis_index("group")
    block_owner, is_live, target, order_rank = routing(keep_flag, destination)
    local_info = lax.dynamic_slice_in_dim(
        jnp.stack([is_live.astype(jnp.int32), target, order_rank]), my_group * IN_DEV, IN_DEV, 1
    )
    peer_ids = jnp.arange(group_count, dtype=jnp.int32)[:, None, None]
    copies = jnp.arange(CAP, dtype=jnp.int32)[None, :, None]
    select = (
        (local_info[0][None, None, :] == 1)
        & (local_info[1][None, None, :] == peer_ids)
        & (local_info[2][None, None, :] == copies)
    )
    rows_flat = values.reshape(IN_DEV, -1)
    packed = jnp.einsum(
        "dcs,sx->dcx", select.astype(jnp.bfloat16), rows_flat, preferred_element_type=jnp.float32
    ).astype(jnp.bfloat16)
    return packed.reshape((group_count, CAP) + values.shape[1:])


def unpack_received(received, keep_flag, destination):
    group_count = lax.axis_size("group")
    my_group = lax.axis_index("group")
    block_owner, is_live, target, order_rank = routing(keep_flag, destination)
    slot_ids = my_group * OUT_DEV + jnp.arange(OUT_DEV, dtype=jnp.int32)
    matched = is_live[None, :] & (destination[None, :] == slot_ids[:, None])
    pair_code = block_owner * CAP + order_rank
    onehot = pair_code[:, None] == jnp.arange(group_count * CAP, dtype=jnp.int32)[None, :]
    select = jnp.dot(matched.astype(jnp.float32), onehot.astype(jnp.float32)).astype(jnp.bfloat16)
    rows_flat = received.reshape(group_count * CAP, -1)
    picked = jnp.dot(select, rows_flat, preferred_element_type=jnp.float32).astype(jnp.bfloat16)
    return (picked.reshape((OUT_DEV,) + received.shape[2:]), matched)


def attend(
    blocks,
    lengths,
    norm_gain,
    w_query,
    key_projection_weight,
    value_projection_weight,
    prompt_key_cache,
    prompt_value_cache,
):
    block_count = blocks.shape[0]
    span_len = blocks.shape[1]
    row_total = block_count * span_len
    gathered = lax.all_gather(blocks, "fsdp", axis=2, tiled=True)
    rows_wide = gathered.reshape(row_total, -1).astype(jnp.float32)
    normalized_input = (
        rows_wide
        * lax.rsqrt(jnp.mean(rows_wide * rows_wide, axis=1, keepdims=True) + EPSILON)
        * norm_gain.astype(jnp.float32)
    ).astype(jnp.bfloat16)
    local_heads = w_query.shape[1] // HEAD_SIZE
    key_value_index = lax.axis_index("fsdp") * local_heads // (QUERY_HEADS // KEY_VALUE_HEADS)
    key_rows = lax.dynamic_slice_in_dim(
        key_projection_weight, key_value_index * HEAD_SIZE, HEAD_SIZE, 1
    )
    value_rows = lax.dynamic_slice_in_dim(
        value_projection_weight, key_value_index * HEAD_SIZE, HEAD_SIZE, 1
    )
    pieces = (
        lax.all_gather(w_query, "group", axis=0, tiled=True),
        lax.all_gather(key_rows, "group", axis=0, tiled=True),
        lax.all_gather(value_rows, "group", axis=0, tiled=True),
    )
    query_vectors = jnp.dot(normalized_input, pieces[0], preferred_element_type=jnp.float32)
    fresh_keys = jnp.dot(normalized_input, pieces[1], preferred_element_type=jnp.float32)
    fresh_values = jnp.dot(normalized_input, pieces[2], preferred_element_type=jnp.float32)
    cosine, sine_table = rope_tables(span_len, PROMPT_TOKENS)
    query_vectors = rotate(
        query_vectors.reshape(block_count, span_len, local_heads, HEAD_SIZE), cosine, sine_table
    ).astype(jnp.bfloat16)
    fresh_keys = (
        rotate(fresh_keys.reshape(block_count, span_len, 1, HEAD_SIZE), cosine, sine_table)
        .reshape(block_count, span_len, HEAD_SIZE)
        .astype(jnp.bfloat16)
    )
    fresh_values = fresh_values.reshape(block_count, span_len, HEAD_SIZE).astype(jnp.bfloat16)
    score_scale = HEAD_SIZE ** (-0.5)
    query_rows = query_vectors.reshape(row_total, local_heads, HEAD_SIZE)
    prompt_keys = lax.dynamic_slice_in_dim(
        prompt_key_cache, key_value_index * HEAD_SIZE, HEAD_SIZE, 1
    )
    prompt_values = lax.dynamic_slice_in_dim(
        prompt_value_cache, key_value_index * HEAD_SIZE, HEAD_SIZE, 1
    )
    pieces = (
        lax.all_gather(prompt_keys, "group", axis=0, tiled=True),
        lax.all_gather(prompt_values, "group", axis=0, tiled=True),
    )
    row_max = jnp.full((row_total, local_heads), MASKED_SCORE, jnp.float32)
    scores = (
        jnp.einsum("rhd,kd->rhk", query_rows, pieces[0], preferred_element_type=jnp.float32)
        * score_scale
    )
    new_max = jnp.maximum(row_max, jnp.max(scores, axis=2))
    powers = jnp.exp(scores - new_max[:, :, None])
    row_sum = jnp.sum(powers, axis=2)
    weighted = jnp.einsum(
        "rhk,kd->rhd", powers.astype(jnp.bfloat16), pieces[1], preferred_element_type=jnp.float32
    )
    row_max, row_sum, weighted = (new_max, row_sum, weighted)
    row_max = row_max.reshape(block_count, span_len, local_heads)
    row_sum = row_sum.reshape(block_count, span_len, local_heads)
    weighted = weighted.reshape(block_count, span_len, local_heads, HEAD_SIZE)
    scores = (
        jnp.einsum("cupy,cly->cupl", query_vectors, fresh_keys, preferred_element_type=jnp.float32)
        * score_scale
    )
    position = jnp.arange(span_len, dtype=jnp.int32)
    allowed = (position[None, None, :] <= position[None, :, None]) & (
        position[None, None, :] < lengths[:, None, None]
    )
    scores = jnp.where(allowed[:, :, None, :], scores, MASKED_SCORE)
    new_max = jnp.maximum(row_max, jnp.max(scores, axis=3))
    powers = jnp.exp(scores - new_max[..., None])
    rescale = jnp.exp(row_max - new_max)
    row_sum = row_sum * rescale + jnp.sum(powers, axis=3)
    weighted = weighted * rescale[..., None] + jnp.einsum(
        "zcmn,znu->zcmu",
        powers.astype(jnp.bfloat16),
        fresh_values,
        preferred_element_type=jnp.float32,
    )
    mixed_out = weighted / row_sum[..., None]
    live_rows = position[None, :] < lengths[:, None]
    mixed_out = jnp.where(live_rows[:, :, None, None], mixed_out, 0.0)
    return mixed_out.reshape(block_count, span_len, local_heads * HEAD_SIZE).astype(jnp.bfloat16)


def body(
    hidden,
    norm_gain,
    w_query,
    key_projection_weight,
    value_projection_weight,
    prompt_key_cache,
    prompt_value_cache,
    keep_flag,
    destination,
    row_counts,
):
    my_group = lax.axis_index("group")
    lengths = lax.dynamic_slice_in_dim(row_counts, my_group * IN_DEV, IN_DEV)
    results = attend(
        hidden,
        lengths,
        norm_gain,
        w_query,
        key_projection_weight,
        value_projection_weight,
        prompt_key_cache,
        prompt_value_cache,
    )
    packed = pack_for_send(results, keep_flag, destination)
    received = lax.all_to_all(packed, "group", split_axis=0, concat_axis=0, tiled=True)
    blocks, matched = unpack_received(received, keep_flag, destination)
    return blocks


def solution(mesh):
    return jax.shard_map(
        body,
        mesh=mesh,
        in_specs=(
            P("group", None, "fsdp"),
            P(),
            P("group", "fsdp"),
            P("group", None),
            P("group", None),
            P("group", None),
            P("group", None),
            P(),
            P(),
            P(),
        ),
        out_specs=P("group", None, "fsdp"),
        check_vma=False,
    )
```

profile of v0, /device:TPU:0, one launch (start us, length us, event | category | flops | bytes accessed | tf_op | source)
XLA Modules:
  0.0 520.2 jit_solution(12677868302810514101)
XLA Ops:
  10.3 1.9 constant_dynamic-slice_fusion
  14.2 9.1 %all_gather.20 = bf16[2048,128]{1,0:T(8,128)(2,1)} all-gather(bf16[512,128]{1,0:T(8,128)(2,1)S(1)} %constant_dynamic-slice_fusion.3), channel_id=1, replica_groups=mesh['group'=4,'fsdp'=8] {'group'}, dimensions={0}, use_global_device_ids=true | all-gather | bytes 655360 | tf_op jit(solution)/shard_map/all_gather | solution.py:151
  24.4 10.9 %all_gather.21 = bf16[2048,128]{1,0:T(8,128)(2,1)} all-gather(bf16[512,128]{1,0:T(8,128)(2,1)S(1)} %constant_dynamic-slice_fusion.2), channel_id=1, replica_groups=mesh['group'=4,'fsdp'=8] {'group'}, dimensions={0}, use_global_device_ids=true | all-gather | bytes 655360 | tf_op jit(solution)/shard_map/all_gather | solution.py:152
  35.8 84.6 %all-gather.7.cloned.1.call-done = bf16[8192,1024]{1,0:T(8,128)(2,1)} async-done(((bf16[2048,1024]{1,0:T(8,128)(2,1)}), bf16[8192,1024]{1,0:T(8,128)(2,1)}) %all-gather.7.cloned.1.call-update) | async-done | bytes 16777232 | tf_op jit(solution)/shard_map/all_gather | solution.py:125
  120.4 21.7 %copy.40 = bf16[1024,8192]{1,0:T(8,128)(2,1)} copy(bf16[1024,8192]{0,1:T(8,128)(2,1)} %bitcast.101) | data formatting | bytes 33554432 | tf_op jit(solution)/shard_map/dot_general | solution.py:129
  142.1 208.1 %all-gather.5.cloned.1.call-done = bf16[8,128,8192]{2,1,0:T(8,128)(2,1)} async-done(((bf16[8,128,1024]{2,1,0:T(8,128)(2,1)}), bf16[8,128,8192]{2,1,0:T(8,128)(2,1)}) %all-gather.5.cloned.1.call-update) | async-done | bytes 16777232 | tf_op jit(solution)/shard_map/all_gather | solution.py:109
  350.2 7.7 %fusion.2 = f32[8,128]{1,0:T(8,128)S(1)} fusion(bf16[8,128,8192]{2,1,0:T(8,128)(2,1)} %all-gather.5.cloned.1.call-done), kind=kLoop, calls=%fused_computation.8 | loop fusion | flops 25164800 | bytes 16781312 | tf_op jit(solution)/shard_map/reduce_sum | solution.py:113
  357.9 3.7 copy-done.2
  361.6 21.2 %fusion.7 = f32[8,128,8,128]{1,3,2,0:T(8,128)S(1)} fusion(bf16[8,128,8192,1]{2,1,0,3:T(8,128)(2,1)} %bitcast.102, bf16[8,128,8192]{2,1,0:T(8,128)(2,1)S(1)} %copy-done.2, f32[8192]{0:T(1024)S(1)} %convert_element_type.59, f32[8,128]{1,0:T(8,128)S(1)} %add_rsqrt_fusion), kind=kOutput, calls=%fused_computation.12 | convolution fusion | flops 17213423616 | bytes 37785600 | tf_op jit(solution)/shard_map/dot_general | solution.py:129
  382.8 1.6 subtract_convert_fusion
  385.5 2.7 copy.58
  388.2 24.8 %multiply_reduce_fusion = (f32[1024,8]{0,1:T(8,128)S(1)}, f32[1024,8,2048]{2,0,1:T(8,128)}) fusion(bf16[2048,128]{1,0:T(8,128)(2,1)} %all_gather.20, bf16[1024,8,64]{2,0,1:T(8,128)(2,1)} %bitcast.104, bf16[1024,8,64]{2,0,1:T(8,128)(2,1)S(1)} %bitcast.103), kind=kOutput, calls=%fused_computation.3 | convolution fusion | flops 4332707840 | bytes 69763072 | tf_op jit(solution)/shard_map/rhd,kd->rhk/dot_general | solution.py:156
  413.1 10.1 %fusion.38 = f32[8,128,1,128]{1,3,0,2:T(8,128)S(1)} fusion(bf16[8192,128]{0,1:T(8,128)(2,1)} %all-gather.9.cloned.1.call-done, bf16[8,128,8192]{2,1,0:T(8,128)(2,1)} %all-gather.5.cloned.1.call-done, f32[8192]{0:T(1024)S(1)} %convert_element_type.59, f32[8,128]{1,0:T(8,128)S(1)} %add_rsqrt_fusion), kind=kOutput, calls=%fused_computation.45 | convolution fusion | flops 2181038080 | bytes 19435520 | tf_op jit(solution)/shard_map/dot_general | solution.py:130
  423.2 2.8 fusion.18
  426.0 21.4 %fusion = f32[1024,8]{0,1:T(8,128)S(1)} fusion(f32[1024,8,2048]{2,0,1:T(8,128)} %get-tuple-element.18, f32[1024,8]{0,1:T(8,128)S(1)} %broadcast_maximum_fusion), kind=kLoop, calls=%fused_computation.4 | loop fusion | flops 50323456 | bytes 67174400 | tf_op jit(solution)/shard_map/reduce_sum | solution.py:161
  447.5 3.3 fusion.19
  450.8 25.3 %fusion.5 = f32[1024,8,128]{2,0,1:T(8,128)} fusion(f32[1024,8,2048]{2,0,1:T(8,128)} %get-tuple-element.18, f32[1024,8]{0,1:T(8,128)S(1)} %broadcast_maximum_fusion, bf16[2048,128]{1,0:T(8,128)(2,1)S(1)} %copy-done.4), kind=kOutput, calls=%fused_computation.11 | convolution fusion | flops 4345298944 | bytes 71860224 | tf_op jit(solution)/shard_map/rhk,kd->rhd/dot_general | solution.py:162
  476.1 12.3 %fusion.17 = bf16[8,128,8,128]{3,1,2,0:T(8,128)(2,1)S(1)} fusion(f32[8,128,8,128]{3,1,0,2:T(8,128)} %bitcast.106, f32[8,128,8,128]{1,3,2,0:T(8,128)} %get-tuple-element.20, f32[8,128,8]{1,2,0:T(8,128)S(1)} %get-tuple-element.5, f32[8,128,8]{1,2,0:T(8,128)S(1)} %bitcast_maximum_fusion, f32[8,128,8]{1,2,0:T(8,128)S(1)} %get-tuple-element.6, ...), kind=kOutput, calls=%fused_computation.22 | convolution fusion | flops 2459041792 | bytes 29627392 | tf_op jit(solution)/shard_map/zcmn,znu->zcmu/dot_general | solution.py:182
  488.5 1.4 copy.84
  489.9 1.4 convolution_convert_fusion.1
  491.3 1.3 copy.86
  492.6 3.6 all-to-all-start
  496.3 14.4 %all-to-all-done = bf16[4,1,128,1024]{3,2,1,0:T(8,128)(2,1)S(1)} async-done(((bf16[4,1,128,1024]{3,2,1,0:T(8,128)(2,1)}), bf16[4,1,128,1024]{3,2,1,0:T(8,128)(2,1)S(1)}, u32[]{:S(2)}, u32[]{:S(2)}) %all-to-all-start) | async-done | bytes 1048608 | tf_op jit(solution)/shard_map/all_to_all | solution.py:219
  512.4 1.3 copy.85
  (72 shorter events, 10.1 us)
Async XLA Ops:
  6.5 7.6 %copy-start = (bf16[512,1024]{1,0:T(8,128)(2,1)S(1)}, bf16[512,1024]{1,0:T(8,128)(2,1)}, u32[]{:S(2)}) copy-start(bf16[512,1024]{1,0:T(8,128)(2,1)} %param.15) | copy-start | bytes 3145732
  6.5 113.8 %all-gather.7.cloned.1.call-start = ((), (), s32[]{:S(2)}) async-start(), calls=%async_computation.2 | async-start | bytes 20971520 | tf_op jit(solution)/shard_map/all_gather | solution.py:125
  7.3 5.0 copy-start.15
  7.3 5.0 copy-start.12
  7.3 16.0 %copy-start.5 = (bf16[8192]{0:T(1024)(128)(2,1)S(1)}, bf16[8192]{0:T(1024)(128)(2,1)}, u32[]{:S(2)}) copy-start(bf16[8192]{0:T(1024)(128)(2,1)} %param.11) | copy-start | bytes 49156
  7.3 16.0 %copy-start.16 = (s32[32]{0:T(128)S(1)}, s32[32]{0:T(128)}, u32[]{:S(2)}) copy-start(s32[32]{0:T(128)} %param.19) | copy-start | bytes 388
  7.3 342.9 %all-gather.5.cloned.1.call-start = ((), (), s32[]{:S(2)}) async-start(), calls=%async_computation.1 | async-start | bytes 18874368 | tf_op jit(solution)/shard_map/all_gather | solution.py:109
  8.1 405.0 %all-gather.9.cloned.1.call-start = ((), (), s32[]{:S(2)}) async-start(), calls=%async_computation.3 | async-start | bytes 2621440 | tf_op jit(solution)/shard_map/all_gather | solution.py:126
  10.2 465.9 %all-gather.11.cloned.1.call-start = ((), (), s32[]{:S(2)}) async-start(), calls=%async_computation.4 | async-start | bytes 2621440 | tf_op jit(solution)/shard_map/all_gather | solution.py:127
  12.3 0.6 copy-start.6
  12.5 129.6 %copy-start.10 = (s32[32]{0:T(128)}, s32[32]{0:T(128)S(1)}, u32[]{:S(2)}) copy-start(s32[32]{0:T(128)S(1)} %convert_reduce_fusion) | copy-start | bytes 388
  350.2 11.4 %copy-start.2 = (bf16[8,128,8192]{2,1,0:T(8,128)(2,1)S(1)}, bf16[8,128,8192]{2,1,0:T(8,128)(2,1)}, u32[]{:S(2)}) copy-start(bf16[8,128,8192]{2,1,0:T(8,128)(2,1)} %all-gather.5.cloned.1.call-done) | copy-start | bytes 50331652
  413.0 10.2 %copy-start.3 = (bf16[8,128,8,64]{1,3,2,0:T(8,128)(2,1)S(1)}, bf16[8,128,8,64]{1,3,2,0:T(8,128)(2,1)}, u32[]{:S(2)}) copy-start(bf16[8,128,8,64]{1,3,2,0:T(8,128)(2,1)} %get-tuple-element.8) | copy-start | bytes 3145732
  447.4 3.4 copy-start.4
  488.4 1.4 copy-start.8
  488.4 1.4 copy-start.9
  488.5 1.4 copy-start.14
  489.8 6.4 %copy-start.11 = (s32[32]{0:T(128)S(1)}, s32[32]{0:T(128)}, u32[]{:S(2)}) copy-start(s32[32]{0:T(128)} %copy-done.10) | copy-start | bytes 388
  489.9 21.6 %copy-start.7 = (pred[32]{0:T(512)(128)(4,1)S(1)}, pred[32]{0:T(512)(128)(4,1)}, u32[]{:S(2)}) copy-start(pred[32]{0:T(512)(128)(4,1)} %copy-done.6) | copy-start | bytes 100
  489.9 21.6 %copy-start.13 = (s32[32]{0:T(128)S(1)}, s32[32]{0:T(128)}, u32[]{:S(2)}) copy-start(s32[32]{0:T(128)} %param.18) | copy-start | bytes 388
  492.6 21.1 %copy-start.1 = (bf16[512,1024]{1,0:T(8,128)(2,1)S(1)}, bf16[512,1024]{1,0:T(8,128)(2,1)}, u32[]{:S(2)}) copy-start(bf16[512,1024]{1,0:T(8,128)(2,1)} %param.15) | copy-start | bytes 3145732
  492.6 18.1 %all-to-all-start = ((bf16[4,1,128,1024]{3,2,1,0:T(8,128)(2,1)}), bf16[4,1,128,1024]{3,2,1,0:T(8,128)(2,1)S(1)}, u32[]{:S(2)}, u32[]{:S(2)}) async-start(bf16[4,1,128,1024]{3,2,1,0:T(8,128)(2,1)} %bitcast.100), calls=%async_computation | async-start | bytes 2097152 | tf_op jit(solution)/shard_map/all_to_all | solution.py:219
Sparse Core Ops, SparseCore 0:
  8.9 111.4 all-gather.6
  122.6 227.5 all-gather.4
  351.8 20.8 all-gather.8
  374.1 22.4 all-gather.10
where the time goes:
time: 521 us; the launch traced here: 520 us
  waiting for transfers between devices  309 us (59%)
  matrix products  98.8 us (19%)
  local copies, waits for them, and re-layouts  40.1 us (8%)
  other arithmetic  35.5 us (7%)
  blocking collectives  20 us (4%)
  between operations  13.5 us (3%)
    all_gather x1, waiting for transfers between devices, attend(): gathered = lax.all_gather(blocks, 'fsdp', axis=2, tiled=True)  208 us
    all_gather x1, waiting for transfers between devices, attend(): lax.all_gather(w_query, 'group', axis=0, tiled=True)  84.6 us
    dot_general x1, matrix products, attend(): jnp.einsum('rhk,kd->rhd', powers.astype(jnp.bfloat16), pieces[1], preferr...  25.3 us
    dot_general x1, matrix products, attend(): jnp.einsum('rhd,kd->rhk', query_rows, pieces[0], preferred_element_type=j...  24.8 us
    dot_general x1, local copies, waits for them, and re-layouts, attend(): jnp.dot(normalized_input, pieces[0], preferred_element_type=jnp.float32)  21.7 us
    reduce_sum x1, other arithmetic, attend(): row_sum = jnp.sum(powers, axis=2)  21.4 us
    dot_general x1, matrix products, attend(): jnp.dot(normalized_input, pieces[0], preferred_element_type=jnp.float32)  21.2 us
    all_to_all x1, waiting for transfers between devices, body(): lax.all_to_all(packed, 'group', split_axis=0, concat_axis=0, tiled=True)  14.4 us
  transfers between devices with their start and end apart: 5, of which 3 were waited for; matrix products, arithmetic and copies ran while one was open for 29% of the time, Pallas kernels for 0%

commit v1 on v0

--- a/solution.py
+++ b/solution.py
@@ -42,55 +42,22 @@
     )
 
 
-def routing(keep_flag, destination):
-    block_total = keep_flag.shape[0]
-    block_index = jnp.arange(block_total, dtype=jnp.int32)
-    block_owner = block_index // IN_DEV
-    is_live = keep_flag == 1
-    target = destination // OUT_DEV
-    earlier = (
-        (block_owner[:, None] == block_owner[None, :])
-        & (target[:, None] == target[None, :])
-        & is_live[None, :]
-        & (block_index[None, :] < block_index[:, None])
-    )
-    order_rank = jnp.sum(earlier.astype(jnp.int32), axis=1)
-    return (block_owner, is_live, target, order_rank)
-
-
 def pack_for_send(values, keep_flag, destination):
     group_count = lax.axis_size("group")
-    my_group = lax.axis_index("group")
-    block_owner, is_live, target, order_rank = routing(keep_flag, destination)
-    local_info = lax.dynamic_slice_in_dim(
-        jnp.stack([is_live.astype(jnp.int32), target, order_rank]), my_group * IN_DEV, IN_DEV, 1
-    )
-    peer_ids = jnp.arange(group_count, dtype=jnp.int32)[:, None, None]
-    copies = jnp.arange(CAP, dtype=jnp.int32)[None, :, None]
-    select = (
-        (local_info[0][None, None, :] == 1)
-        & (local_info[1][None, None, :] == peer_ids)
-        & (local_info[2][None, None, :] == copies)
-    )
-    rows_flat = values.reshape(IN_DEV, -1)
-    packed = jnp.einsum(
-        "dcs,sx->dcx", select.astype(jnp.bfloat16), rows_flat, preferred_element_type=jnp.float32
-    ).astype(jnp.bfloat16)
-    return packed.reshape((group_count, CAP) + values.shape[1:])
-
-
-def unpack_received(received, keep_flag, destination):
-    group_count = lax.axis_size("group")
-    my_group = lax.axis_index("group")
-    block_owner, is_live, target, order_rank = routing(keep_flag, destination)
-    slot_ids = my_group * OUT_DEV + jnp.arange(OUT_DEV, dtype=jnp.int32)
-    matched = is_live[None, :] & (destination[None, :] == slot_ids[:, None])
-    pair_code = block_owner * CAP + order_rank
-    onehot = pair_code[:, None] == jnp.arange(group_count * CAP, dtype=jnp.int32)[None, :]
-    select = jnp.dot(matched.astype(jnp.float32), onehot.astype(jnp.float32)).astype(jnp.bfloat16)
-    rows_flat = received.reshape(group_count * CAP, -1)
-    picked = jnp.dot(select, rows_flat, preferred_element_type=jnp.float32).astype(jnp.bfloat16)
-    return (picked.reshape((OUT_DEV,) + received.shape[2:]), matched)
+    first = lax.axis_index("group") * IN_DEV
+    keep = lax.dynamic_slice_in_dim(keep_flag, first, IN_DEV) == 1
+    target = lax.dynamic_slice_in_dim(destination, first, IN_DEV) // OUT_DEV
+    peers = jnp.arange(group_count, dtype=jnp.int32)
+    chosen = jnp.argmax(keep[None, :] & (target[None, :] == peers[:, None]), axis=1)
+    return jnp.stack(
+        [lax.dynamic_index_in_dim(values, chosen[d], 0, False) for d in range(group_count)]
+    )
+
+
+def slot_sources(keep_flag, destination):
+    slots = lax.axis_index("group") * OUT_DEV + jnp.arange(OUT_DEV, dtype=jnp.int32)
+    matched = (keep_flag[None, :] == 1) & (destination[None, :] == slots[:, None])
+    return jnp.argmax(matched, axis=1).astype(jnp.int32)
 
 
 def attend(
@@ -203,11 +170,16 @@
     destination,
     row_counts,
 ):
-    my_group = lax.axis_index("group")
-    lengths = lax.dynamic_slice_in_dim(row_counts, my_group * IN_DEV, IN_DEV)
-    results = attend(
-        hidden,
-        lengths,
+    sources = slot_sources(keep_flag, destination)
+    packed = pack_for_send(hidden, keep_flag, destination)
+    received = lax.all_to_all(packed, "group", split_axis=0, concat_axis=0, tiled=True)
+    owners = sources // IN_DEV
+    blocks = jnp.stack(
+        [lax.dynamic_index_in_dim(received, owners[o], 0, False) for o in range(OUT_DEV)]
+    )
+    return attend(
+        blocks,
+        row_counts[sources],
         norm_gain,
         w_query,
         key_projection_weight,
@@ -215,10 +187,6 @@
         prompt_key_cache,
         prompt_value_cache,
     )
-    packed = pack_for_send(results, keep_flag, destination)
-    received = lax.all_to_all(packed, "group", split_axis=0, concat_axis=0, tiled=True)
-    blocks, matched = unpack_received(received, keep_flag, destination)
-    return blocks
 
 
 def solution(mesh):

time: 521 us -> 415 us (0.80)
  waiting for transfers between devices: 309 us -> 246 us
  matrix products: 98.8 us -> 58.2 us
  between operations: 13.5 us -> 28.5 us
  other arithmetic: 35.5 us -> 28.1 us
  local copies, waits for them, and re-layouts: 40.1 us -> 34.2 us
  blocking collectives: 20 us -> 14.2 us
    all_gather x1, waiting for transfers between devices: 208 us -> 105 us  [attend(): gathered = lax.all_gather(blocks, 'fsdp', axis=2, tiled=True)]
    all_gather x1, waiting for transfers between devices: 0.02 us -> 17.2 us  [attend(): lax.all_gather(key_rows, 'group', axis=0, tiled=True)]
    all_gather x1, waiting for transfers between devices: 0.01 us -> 17.2 us  [attend(): lax.all_gather(value_rows, 'group', axis=0, tiled=True)]
    all_gather x1, waiting for transfers between devices: 84.6 us -> 101 us  [attend(): lax.all_gather(w_query, 'group', axis=0, tiled=True)]
    dot_general x1, matrix products: 25.3 us -> 13.4 us  [attend(): jnp.einsum('rhk,kd->rhd', powers.astype(jnp.bfloat16), pieces[1], preferr...]
    dot_general x1, matrix products: 24.8 us -> 13.2 us  [attend(): jnp.einsum('rhd,kd->rhk', query_rows, pieces[0], preferred_element_type=j...]
    dot_general x1, matrix products: 12.3 us -> 3.2 us  [attend(): jnp.einsum('zcmn,znu->zcmu', powers.astype(jnp.bfloat16), fresh_values, p...]
    all_to_all x1, waiting for transfers between devices: 14.4 us -> 5.43 us  [body(): lax.all_to_all(packed, 'group', split_axis=0, concat_axis=0, tiled=True)]
  transfers between devices with their start and end apart: 5 -> 5, of which waited for: 3 -> 5; matrix products, arithmetic and copies ran while one was open for 29% -> 6% of each run, Pallas kernels for 0% -> 0%
where the time goes in v1:
time: 415 us; the launch traced here: 414 us
  waiting for transfers between devices  246 us (59%)
  matrix products  58.2 us (14%)
  local copies, waits for them, and re-layouts  34.2 us (8%)
  between operations  28.5 us (7%)
  other arithmetic  28.1 us (7%)
  blocking collectives  14.2 us (3%)
  starting transfers between devices  4.33 us (1%)
    all_gather x1, waiting for transfers between devices, attend(): gathered = lax.all_gather(blocks, 'fsdp', axis=2, tiled=True)  105 us
    all_gather x1, waiting for transfers between devices, attend(): lax.all_gather(w_query, 'group', axis=0, tiled=True)  101 us
    dot_general x1, local copies, waits for them, and re-layouts, attend(): jnp.dot(normalized_input, pieces[0], preferred_element_type=jnp.float32)  20.7 us
    all_gather x1, waiting for transfers between devices, attend(): lax.all_gather(key_rows, 'group', axis=0, tiled=True)  17.2 us
    all_gather x1, waiting for transfers between devices, attend(): lax.all_gather(value_rows, 'group', axis=0, tiled=True)  17.2 us
    reduce_sum x1, other arithmetic, attend(): row_sum = jnp.sum(powers, axis=2)  14.1 us
    dot_general x1, matrix products, attend(): jnp.einsum('rhk,kd->rhd', powers.astype(jnp.bfloat16), pieces[1], preferr...  13.4 us
    dot_general x1, matrix products, attend(): jnp.dot(normalized_input, pieces[0], preferred_element_type=jnp.float32)  13.2 us
  transfers between devices with their start and end apart: 5, of which 5 were waited for; matrix products, arithmetic and copies ran while one was open for 6% of the time, Pallas kernels for 0%

profile of v1, /device:TPU:0, one launch (start us, length us, event | category | flops | bytes accessed | tf_op | source)
XLA Modules:
  0.0 414.0 jit_solution(11931407128112068972)
XLA Ops:
  17.0 1.3 constant_dynamic-slice_fusion.11
  19.4 4.2 %all-to-all-start = ((bf16[4,128,1024]{2,1,0:T(8,128)(2,1)}), bf16[4,128,1024]{2,1,0:T(8,128)(2,1)S(1)}, u32[]{:S(2)}, u32[]{:S(2)}) async-start(bf16[4,128,1024]{2,1,0:T(8,128)(2,1)} %pad_maximum_fusion), calls=%async_computation | async-start | bytes 2097152 | tf_op jit(solution)/shard_map/all_to_all | solution.py:175
  32.6 5.4 %all-to-all-done = bf16[4,128,1024]{2,1,0:T(8,128)(2,1)S(1)} async-done(((bf16[4,128,1024]{2,1,0:T(8,128)(2,1)}), bf16[4,128,1024]{2,1,0:T(8,128)(2,1)S(1)}, u32[]{:S(2)}, u32[]{:S(2)}) %all-to-all-start) | async-done | bytes 1048608 | tf_op jit(solution)/shard_map/all_to_all | solution.py:175
  41.5 1.9 constant_dynamic-slice_fusion
  45.7 7.0 %all_gather.21 = bf16[2048,128]{1,0:T(8,128)(2,1)} all-gather(bf16[512,128]{1,0:T(8,128)(2,1)S(1)} %constant_dynamic-slice_fusion.2), channel_id=1, replica_groups=mesh['group'=4,'fsdp'=8] {'group'}, dimensions={0}, use_global_device_ids=true | all-gather | bytes 655360 | tf_op jit(solution)/shard_map/all_gather | solution.py:119
  52.7 7.3 %all_gather.20 = bf16[2048,128]{1,0:T(8,128)(2,1)S(1)} all-gather(bf16[512,128]{1,0:T(8,128)(2,1)S(1)} %constant_dynamic-slice_fusion.3), channel_id=1, replica_groups=mesh['group'=4,'fsdp'=8] {'group'}, dimensions={0}, use_global_device_ids=true | all-gather | bytes 655360 | tf_op jit(solution)/shard_map/all_gather | solution.py:118
  60.4 105.0 %all-gather.5.cloned.1.call-done = bf16[4,128,8192]{2,1,0:T(8,128)(2,1)} async-done(((bf16[4,128,1024]{2,1,0:T(8,128)(2,1)}), bf16[4,128,8192]{2,1,0:T(8,128)(2,1)}) %all-gather.5.cloned.1.call-update) | async-done | bytes 8388624 | tf_op jit(solution)/shard_map/all_gather | solution.py:76
  165.4 5.1 %fusion.2 = f32[4,128]{1,0:T(4,128)S(1)} fusion(bf16[4,128,8192]{2,1,0:T(8,128)(2,1)} %all-gather.5.cloned.1.call-done), kind=kLoop, calls=%fused_computation.7 | loop fusion | flops 12582400 | bytes 8390656 | tf_op jit(solution)/shard_map/reduce_sum | solution.py:80
  170.5 17.2 %all-gather.9.cloned.1.call-done = bf16[8192,128]{0,1:T(8,128)(2,1)} async-done(((bf16[2048,128]{0,1:T(8,128)(2,1)}), bf16[8192,128]{0,1:T(8,128)(2,1)}) %all-gather.9.cloned.1.call-update) | async-done | bytes 2097168 | tf_op jit(solution)/shard_map/all_gather | solution.py:93
  187.7 7.0 %fusion.19 = f32[4,128,1,128]{1,3,0,2:T(8,128)S(1)} fusion(bf16[8192,128]{0,1:T(8,128)(2,1)} %all-gather.9.cloned.1.call-done, bf16[4,128,8192]{2,1,0:T(8,128)(2,1)} %all-gather.5.cloned.1.call-done, f32[8192]{0:T(1024)S(1)} %convert_element_type.38, f32[4,128]{1,0:T(4,128)S(1)} %add_rsqrt_fusion), kind=kOutput, calls=%fused_computation.23 | convolution fusion | flops 1090519040 | bytes 10782720 | tf_op jit(solution)/shard_map/dot_general | solution.py:97
  194.7 17.2 %all-gather.11.cloned.1.call-done = bf16[8192,128]{1,0:T(8,128)(2,1)} async-done(((bf16[2048,128]{1,0:T(8,128)(2,1)}), bf16[8192,128]{1,0:T(8,128)(2,1)}) %all-gather.11.cloned.1.call-update) | async-done | bytes 2097168 | tf_op jit(solution)/shard_map/all_gather | solution.py:94
  211.9 6.4 %fusion.29 = bf16[4,128,128,1]{2,1,3,0:T(8,128)(2,1)S(1)} fusion(bf16[8192,128]{1,0:T(8,128)(2,1)} %all-gather.11.cloned.1.call-done, bf16[4,128,8192]{2,1,0:T(8,128)(2,1)} %all-gather.5.cloned.1.call-done, f32[8192]{0:T(1024)S(1)} %convert_element_type.38, f32[4,128]{1,0:T(4,128)S(1)} %add_rsqrt_fusion), kind=kOutput, calls=%fused_computation.25 | convolution fusion | flops 1090584576 | bytes 10651648 | tf_op jit(solution)/shard_map/dot_general | solution.py:98
  218.3 101.0 %all-gather.7.cloned.1.call-done = bf16[8192,1024]{1,0:T(8,128)(2,1)} async-done(((bf16[2048,1024]{1,0:T(8,128)(2,1)}), bf16[8192,1024]{1,0:T(8,128)(2,1)}) %all-gather.7.cloned.1.call-update) | async-done | bytes 16777232 | tf_op jit(solution)/shard_map/all_gather | solution.py:92
  319.3 20.7 %copy.29 = bf16[1024,8192]{1,0:T(8,128)(2,1)} copy(bf16[1024,8192]{0,1:T(8,128)(2,1)} %bitcast.70) | data formatting | bytes 33554432 | tf_op jit(solution)/shard_map/dot_general | solution.py:96
  340.0 13.2 %fusion.7 = f32[4,128,8,128]{1,3,2,0:T(8,128)S(1)} fusion(bf16[8,128,8192,1]{2,1,0,3:T(8,128)(2,1)} %bitcast.71, bf16[4,128,8192]{2,1,0:T(8,128)(2,1)} %all-gather.5.cloned.1.call-done, f32[8192]{0:T(1024)S(1)} %convert_element_type.38, f32[4,128]{1,0:T(4,128)S(1)} %add_rsqrt_fusion), kind=kOutput, calls=%fused_computation.11 | convolution fusion | flops 8606711808 | bytes 27297792 | tf_op jit(solution)/shard_map/dot_general | solution.py:96
  354.8 1.5 copy.47
  356.4 13.2 %multiply_reduce_fusion = (f32[512,8]{0,1:T(8,128)S(1)}, f32[512,8,2048]{2,0,1:T(8,128)}) fusion(bf16[2048,128]{1,0:T(8,128)(2,1)S(1)} %all_gather.20, bf16[512,8,64]{2,0,1:T(8,128)(2,1)S(1)} %bitcast.74, bf16[512,8,64]{2,0,1:T(8,128)(2,1)S(1)} %bitcast.73), kind=kOutput, calls=%fused_computation.2 | convolution fusion | flops 2166353920 | bytes 35143680 | tf_op jit(solution)/shard_map/rhd,kd->rhk/dot_general | solution.py:123
  369.6 1.8 fusion.16
  371.4 14.1 %fusion = f32[512,8]{0,1:T(8,128)S(1)} fusion(f32[512,8,2048]{2,0,1:T(8,128)} %get-tuple-element.36, f32[512,8]{0,1:T(8,128)S(1)} %broadcast_maximum_fusion), kind=kLoop, calls=%fused_computation.3 | loop fusion | flops 25161728 | bytes 33587200 | tf_op jit(solution)/shard_map/reduce_sum | solution.py:128
  385.5 13.4 %fusion.5 = f32[512,8,128]{2,0,1:T(8,128)S(1)} fusion(f32[512,8,2048]{2,0,1:T(8,128)} %get-tuple-element.36, f32[512,8]{0,1:T(8,128)S(1)} %broadcast_maximum_fusion, bf16[2048,128]{1,0:T(8,128)(2,1)S(1)} %copy-done.3), kind=kOutput, calls=%fused_computation.10 | convolution fusion | flops 2172649472 | bytes 36192256 | tf_op jit(solution)/shard_map/rhk,kd->rhd/dot_general | solution.py:129
  398.9 1.9 copy.37
  400.8 2.1 fusion.17
  402.9 3.2 select_convert_fusion
  406.1 1.3 copy.40
  (56 shorter events, 13.2 us)
Async XLA Ops:
  6.5 38.2 %copy-start = (bf16[512,1024]{1,0:T(8,128)(2,1)S(1)}, bf16[512,1024]{1,0:T(8,128)(2,1)}, u32[]{:S(2)}) copy-start(bf16[512,1024]{1,0:T(8,128)(2,1)} %param.15) | copy-start | bytes 3145732
  6.5 17.0 %copy-start.7 = (s32[32]{0:T(128)S(1)}, s32[32]{0:T(128)}, u32[]{:S(2)}) copy-start(s32[32]{0:T(128)} %param.17) | copy-start | bytes 388
  6.5 17.1 %copy-start.6 = (s32[32]{0:T(128)S(1)}, s32[32]{0:T(128)}, u32[]{:S(2)}) copy-start(s32[32]{0:T(128)} %param.18) | copy-start | bytes 388
  19.4 18.7 %all-to-all-start = ((bf16[4,128,1024]{2,1,0:T(8,128)(2,1)}), bf16[4,128,1024]{2,1,0:T(8,128)(2,1)S(1)}, u32[]{:S(2)}, u32[]{:S(2)}) async-start(bf16[4,128,1024]{2,1,0:T(8,128)(2,1)} %pad_maximum_fusion), calls=%async_computation | async-start | bytes 2097152 | tf_op jit(solution)/shard_map/all_to_all | solution.py:175
  23.6 141.8 %all-gather.5.cloned.1.call-start = ((), (), s32[]{:S(2)}) async-start(), calls=%async_computation.1 | async-start | bytes 9437184 | tf_op jit(solution)/shard_map/all_gather | solution.py:76
  39.2 148.5 %all-gather.9.cloned.1.call-start = ((), (), s32[]{:S(2)}) async-start(), calls=%async_computation.3 | async-start | bytes 2621440 | tf_op jit(solution)/shard_map/all_gather | solution.py:93
  39.3 4.7 %copy-start.5 = (bf16[8192]{0:T(1024)(128)(2,1)S(1)}, bf16[8192]{0:T(1024)(128)(2,1)}, u32[]{:S(2)}) copy-start(bf16[8192]{0:T(1024)(128)(2,1)} %param.11) | copy-start | bytes 49156
  39.3 4.7 %copy-start.2 = (s32[32]{0:T(128)S(1)}, s32[32]{0:T(128)}, u32[]{:S(2)}) copy-start(s32[32]{0:T(128)} %param.19) | copy-start | bytes 388
  41.5 170.4 %all-gather.11.cloned.1.call-start = ((), (), s32[]{:S(2)}) async-start(), calls=%async_computation.4 | async-start | bytes 2621440 | tf_op jit(solution)/shard_map/all_gather | solution.py:94
  43.4 275.8 %all-gather.7.cloned.1.call-start = ((), (), s32[]{:S(2)}) async-start(), calls=%async_computation.2 | async-start | bytes 20971520 | tf_op jit(solution)/shard_map/all_gather | solution.py:92
  356.4 13.2 %copy-start.4 = (bf16[4,128,8,64]{1,3,2,0:T(8,128)(2,1)S(1)}, bf16[4,128,8,64]{1,3,2,0:T(8,128)(2,1)}, u32[]{:S(2)}) copy-start(bf16[4,128,8,64]{1,3,2,0:T(8,128)(2,1)} %get-tuple-element.12) | copy-start | bytes 1572868
  371.4 14.1 %copy-start.3 = (bf16[2048,128]{1,0:T(8,128)(2,1)S(1)}, bf16[2048,128]{1,0:T(8,128)(2,1)}, u32[]{:S(2)}) copy-start(bf16[2048,128]{1,0:T(8,128)(2,1)} %all_gather.21) | copy-start | bytes 1572868
  402.9 4.5 %copy-start.1 = (bf16[512,1024]{1,0:T(8,128)(2,1)S(1)}, bf16[512,1024]{1,0:T(8,128)(2,1)}, u32[]{:S(2)}) copy-start(bf16[512,1024]{1,0:T(8,128)(2,1)} %param.15) | copy-start | bytes 3145732
Sparse Core Ops, SparseCore 0:
  39.4 125.9 all-gather.4
  166.9 20.7 all-gather.8
  189.3 22.5 all-gather.10
  213.3 105.9 all-gather.6

commit v2 on v1

v2 whole, which is shorter than its diff:
```python
import functools
import math

import jax
import jax.numpy as jnp
from jax import lax
from jax.experimental import pallas as pl
from jax.experimental.pallas import tpu as pltpu
from jax.sharding import PartitionSpec as P

QUERY_HEADS = 64
KEY_VALUE_HEADS = 8
HEAD_SIZE = 128
PROMPT_TOKENS = 2048
IN_DEV = 8
CAP = 1
OUT_DEV = 4


EPSILON = 1e-05
ROPE_THETA = 500000.0
CONTEXT_BASE = 8192.0
STRETCH = 8.0
MASKED_SCORE = -1e30


def rope_tables(length, offset):
    half_dim = HEAD_SIZE // 2
    base_rate = ROPE_THETA ** (-(jnp.arange(half_dim, dtype=jnp.float32) * 2.0 / HEAD_SIZE))
    ratio = CONTEXT_BASE * base_rate / (2.0 * jnp.pi)
    smooth = jnp.clip((ratio - 1.0) / 3.0, 0.0, 1.0)
    inverse_rate = (1.0 - smooth) * base_rate / STRETCH + smooth * base_rate
    token_positions = jnp.arange(length, dtype=jnp.float32) + offset
    angles = token_positions[:, None] * inverse_rate[None, :]
    return (jnp.cos(angles), jnp.sin(angles))


CHUNKS = 4
ROW_TILE = 16
COLUMN_TILE = 2 * HEAD_SIZE
MESH = pl.DeviceIdType.MESH


def project_kernel(
    shape,
    keep_ref,
    dest_ref,
    hidden_ref,
    gain_ref,
    wq_ref,
    wk_ref,
    wv_ref,
    kc_ref,
    vc_ref,
    acc_ref,
    cache_out_ref,
    outbox,
    inbox,
    x_all,
    x_norm,
    w_all,
    cache,
    local_sem,
    inbox_send,
    inbox_recv,
    x_send,
    x_recv,
    w_send,
    w_recv,
):
    groups, shards, lines, width = shape
    columns = shards // lines
    chips = groups // 2
    features = hidden_ref.shape[2]
    span = hidden_ref.shape[1]
    depth = wq_ref.shape[0]
    chunk = depth // CHUNKS
    heads = wq_ref.shape[1] // HEAD_SIZE
    group = lax.axis_index("group")
    shard = lax.axis_index("fsdp")
    chip, core = group // 2, group % 2
    col, line = shard // lines, shard % lines
    head = shard * heads // (QUERY_HEADS // KEY_VALUE_HEADS)
    head_cols = pl.ds(pl.multiple_of(head * HEAD_SIZE, HEAD_SIZE), HEAD_SIZE)

    local = []
    for c in range(CHUNKS):
        rows = pl.ds(c * chunk, chunk)
        mine = w_all.at[group, c]
        copies = [
            pltpu.make_async_copy(
                wq_ref.at[rows, pl.ds(n * HEAD_SIZE, HEAD_SIZE)], mine.at[n], local_sem.at[c, n]
            )
            for n in range(heads)
        ]
        for n, ref in ((heads, wk_ref), (heads + 1, wv_ref)):
            copies.append(
                pltpu.make_async_copy(ref.at[rows, head_cols], mine.at[n], local_sem.at[c, n])
            )
        local.append(copies)
    local.append(
        [
            pltpu.make_async_copy(
                ref.at[:, head_cols], cache.at[group, n], local_sem.at[CHUNKS, n]
            )
            for n, ref in enumerate((kc_ref, vc_ref))
        ]
    )
    for copies in local:
        for copy in copies:
            copy.start()

    x_hops = [
        (col < columns - 1, shard + lines),
        (col > 0, shard - lines),
        (line < lines - 1, shard + 1),
        (line > 0, shard - 1),
    ]
    w_hops = [(chip < chips - 1, group + 2), (chip > 0, group - 2)]
    partner = chip * 2 + 1 - core

    barrier = pltpu.get_barrier_semaphore()
    for j in range(1, groups):
        pl.semaphore_signal(
            barrier, inc=1, device_id={"group": (group + j) % groups}, device_id_type=MESH
        )
    for valid, near in x_hops:

        @pl.when(valid)
        def _(near=near):
            pl.semaphore_signal(barrier, inc=1, device_id={"fsdp": near}, device_id_type=MESH)

    near_count = sum(jnp.where(valid, 1, 0) for valid, _ in x_hops)
    pl.semaphore_wait(barrier, groups - 1 + near_count)

    first = group * IN_DEV

    def chosen(target):
        index = jnp.int32(0)
        for b in range(IN_DEV):
            hit = (keep_ref[first + b] == 1) & (lax.div(dest_ref[first + b], OUT_DEV) == target)
            index = jnp.where(hit, b, index)
        return index

    posts = []
    for j in range(groups - 1, 0, -1):
        peer = (group + j) % groups
        outbox[j - 1] = hidden_ref[chosen(peer)]
        post = pltpu.make_async_remote_copy(
            src_ref=outbox.at[j - 1],
            dst_ref=inbox.at[group],
            send_sem=inbox_send.at[j - 1],
            recv_sem=inbox_recv.at[group],
            device_id={"group": peer},
            device_id_type=MESH,
        )
        post.start()
        posts.append(post)
    inbox[group] = hidden_ref[chosen(group)]

    sends = []

    def x_copy(unit, hop):
        return pltpu.make_async_remote_copy(
            src_ref=x_all.at[unit],
            dst_ref=x_all.at[unit],
            send_sem=x_send.at[unit, hop],
            recv_sem=x_recv.at[unit],
            device_id={"fsdp": x_hops[hop][1]},
            device_id_type=MESH,
        )

    def x_arrival(unit):
        return pltpu.make_async_remote_copy(
            src_ref=x_all.at[unit],
            dst_ref=x_all.at[unit],
            send_sem=x_send.at[unit, 0],
            recv_sem=x_recv.at[unit],
            device_id={"fsdp": (shard + 1) % shards},
            device_id_type=MESH,
        )

    def w_copy(unit, c, hop):
        ref = cache.at[unit] if c == CHUNKS else w_all.at[unit, c]
        return pltpu.make_async_remote_copy(
            src_ref=ref,
            dst_ref=ref,
            send_sem=w_send.at[unit, c, hop],
            recv_sem=w_recv.at[unit, c],
            device_id={"group": partner if hop == 2 else w_hops[hop][1]},
            device_id_type=MESH,
        )

    def launch(copy, when):
        @pl.when(when)
        def _():
            copy.start()

        sends.append((copy, when))

    always = group >= 0
    order = [CHUNKS] + list(range(CHUNKS))
    for c in order:
        for copy in local[c]:
            copy.wait()
        for hop in (0, 1):
            launch(w_copy(group, c, hop), w_hops[hop][0])
        launch(w_copy(group, c, 2), always)

    for j in range(1, groups):
        source = (group + j) % groups
        pltpu.make_async_remote_copy(
            src_ref=inbox.at[source],
            dst_ref=inbox.at[source],
            send_sem=inbox_send.at[j - 1],
            recv_sem=inbox_recv.at[source],
            device_id={"group": source},
            device_id_type=MESH,
        ).wait_recv()
    for o in range(OUT_DEV):
        slot = group * OUT_DEV + o

        def find(b, owner):
            hit = (keep_ref[b] == 1) & (dest_ref[b] == slot)
            return jnp.where(hit, lax.div(b, jnp.int32(IN_DEV)), owner)

        owner = lax.fori_loop(0, groups * IN_DEV, find, jnp.int32(0))
        x_all[shard, pl.ds(o * span, span), :] = inbox[owner]

    for hop in range(4):
        launch(x_copy(shard, hop), x_hops[hop][0])

    def x_column(step):
        for hop, sign in ((0, 1), (1, -1)):
            source = col - sign * step
            there = (source >= 0) & (source < columns)
            unit = source * lines + line

            @pl.when(there)
            def _(unit=unit):
                x_arrival(unit).wait_recv()

            if step < columns - 1:
                launch(x_copy(unit, hop), there & x_hops[hop][0])
            for side in (2, 3):
                launch(x_copy(unit, side), there & x_hops[side][0])

    def x_line(step):
        for hop, sign in ((2, 1), (3, -1)):
            source = line - sign * step
            there = (source >= 0) & (source < lines)
            for k in range(columns):
                unit = k * lines + source

                @pl.when(there)
                def _(unit=unit):
                    x_arrival(unit).wait_recv()

                if step < lines - 1:
                    launch(x_copy(unit, hop), there & x_hops[hop][0])

    def w_chip(step, c):
        for hop, sign in ((0, 1), (1, -1)):
            source = chip - sign * step
            there = (source >= 0) & (source < chips)
            unit = source * 2 + core

            @pl.when(there)
            def _(unit=unit):
                w_copy(unit, c, 2).wait_recv()

            if step < chips - 1:
                launch(w_copy(unit, c, hop), there & w_hops[hop][0])
            launch(w_copy(unit, c, 2), there)

    w_events = [(step, c) for step in range(1, chips) for c in order]
    w_chip(*w_events.pop(0))
    for step in range(1, columns):
        x_column(step)
        if len(w_events) > 2:
            w_chip(*w_events.pop(0))
    for step in range(1, lines):
        x_line(step)

    def normalize(i, carry):
        rows = pl.ds(pl.multiple_of(i * ROW_TILE, ROW_TILE), ROW_TILE)
        total = jnp.zeros((ROW_TILE, features), jnp.float32)
        for f in range(shards):
            values = x_all[f, rows, :].astype(jnp.float32)
            total = total + values * values
        mean = jnp.sum(total, axis=1, keepdims=True) / width
        factor = lax.rsqrt(mean + EPSILON)
        for f in range(shards):
            values = x_all[f, rows, :].astype(jnp.float32)
            x_norm[f, rows, :] = (values * factor * gain_ref[pl.ds(f, 1), :]).astype(jnp.bfloat16)
        return carry

    lax.fori_loop(0, OUT_DEV * span // ROW_TILE, normalize, 0)
    acc_ref[...] = jnp.zeros_like(acc_ref)

    def multiply(unit, c):
        block = unit * (depth // features) + c * chunk // features
        inner = pl.ds(c * chunk % features, chunk)

        def tile(n, carry):
            cols = pl.ds(pl.multiple_of(n * COLUMN_TILE, COLUMN_TILE), COLUMN_TILE)
            acc_ref[:, cols] += jnp.dot(
                x_norm[block, :, inner],
                jnp.concatenate([w_all[unit, c, 2 * n], w_all[unit, c, 2 * n + 1]], axis=1),
                preferred_element_type=jnp.float32,
            )
            return carry

        lax.fori_loop(0, acc_ref.shape[1] // COLUMN_TILE, tile, 0)

    def from_partner(unit, c):
        w_copy(unit, c, 2).wait_recv()

    while w_events:
        w_chip(*w_events.pop(0))
    for d in range(chips):
        for c in order:
            from_partner((chip + d) % chips * 2 + 1 - core, c)
    for unit in range(groups):
        for c in range(CHUNKS):
            multiply(unit, c)
    result = pltpu.make_async_copy(cache, cache_out_ref, local_sem.at[CHUNKS, 2])
    result.start()
    for post in posts:
        post.wait_send()
    for copy, when in sends:

        @pl.when(when)
        def _(copy=copy):
            copy.wait_send()

    result.wait()


def project(shards, groups, hidden, norm_gain, w_query, wk, wv, kc, vc, keep_flag, destination):
    blocks, span, features = hidden.shape
    depth, q_width = w_query.shape
    width = norm_gain.shape[0]
    lines = math.isqrt(shards // 2)
    rows = OUT_DEV * span
    out_width = q_width + 2 * HEAD_SIZE
    cached = kc.shape[0]
    smem = pl.BlockSpec(memory_space=pltpu.SMEM)
    vmem = pl.BlockSpec(memory_space=pltpu.VMEM)
    anywhere = pl.BlockSpec(memory_space=pl.ANY)
    dma = pltpu.SemaphoreType.DMA
    return pl.pallas_call(
        functools.partial(project_kernel, (groups, shards, lines, width)),
        out_shape=(
            jax.ShapeDtypeStruct((rows, out_width), jnp.float32),
            jax.ShapeDtypeStruct((groups, 2, cached, HEAD_SIZE), jnp.bfloat16),
        ),
        in_specs=[smem, smem, vmem, vmem] + [anywhere] * 5,
        out_specs=(vmem, anywhere),
        scratch_shapes=[
            pltpu.VMEM((groups - 1, span, features), jnp.bfloat16),
            pltpu.VMEM((groups, span, features), jnp.bfloat16),
            pltpu.VMEM((shards, rows, features), jnp.bfloat16),
            pltpu.VMEM((shards, rows, features), jnp.bfloat16),
            pltpu.VMEM((groups, CHUNKS, out_width // HEAD_SIZE, depth // CHUNKS, HEAD_SIZE), jnp.bfloat16),
            pltpu.VMEM((groups, 2, cached, HEAD_SIZE), jnp.bfloat16),
            dma((CHUNKS + 1, out_width // HEAD_SIZE)),
            dma((groups - 1,)),
            dma((groups,)),
            dma((shards, 4)),
            dma((shards,)),
            dma((groups, CHUNKS + 1, 3)),
            dma((groups, CHUNKS + 1)),
        ],
        compiler_params=pltpu.CompilerParams(
            collective_id=0, has_side_effects=True, vmem_limit_bytes=58 * 1024 * 1024
        ),
        cost_estimate=pl.CostEstimate(
            flops=2 * rows * width * out_width, bytes_accessed=depth * out_width * 2, transcendentals=0
        ),
        name="gather_and_project",
    )(
        keep_flag,
        destination,
        hidden,
        norm_gain.astype(jnp.float32).reshape(shards, features),
        w_query,
        wk,
        wv,
        kc,
        vc,
    )


def attention_kernel(
    keep_ref, dest_ref, counts_ref, cos_ref, sin_ref, q_ref, k_ref, v_ref, cache_ref, out_ref
):
    slot = lax.axis_index("group") * OUT_DEV + pl.program_id(0)

    def find(b, length):
        hit = (keep_ref[b] == 1) & (dest_ref[b] == slot)
        return jnp.where(hit, counts_ref[b], length)

    length = lax.fori_loop(0, keep_ref.shape[0], find, jnp.int32(0))
    cosine, sine = cos_ref[...], sin_ref[...]

    def turn(values):
        return (values * cosine + pltpu.roll(values, HEAD_SIZE // 2, 1) * sine).astype(jnp.bfloat16)

    span = q_ref.shape[0]
    heads = q_ref.shape[1] // HEAD_SIZE
    queries = jnp.concatenate(
        [turn(q_ref[:, h * HEAD_SIZE : (h + 1) * HEAD_SIZE]) for h in range(heads)], axis=0
    )
    keys = turn(k_ref[...])
    values = v_ref[...].astype(jnp.bfloat16)
    contract = (((1,), (1,)), ((), ()))
    tokens = cache_ref.shape[0] * cache_ref.shape[2]
    prompt_keys = cache_ref[:, 0].reshape(tokens, HEAD_SIZE)
    prompt_values = cache_ref[:, 1].reshape(tokens, HEAD_SIZE)
    cached = lax.dot_general(
        queries, prompt_keys, contract, preferred_element_type=jnp.float32
    )
    fresh = lax.dot_general(queries, keys, contract, preferred_element_type=jnp.float32)
    row = lax.broadcasted_iota(jnp.int32, fresh.shape, 0) % span
    column = lax.broadcasted_iota(jnp.int32, fresh.shape, 1)
    fresh = jnp.where((column <= row) & (column < length), fresh, MASKED_SCORE)
    top = jnp.maximum(
        jnp.max(cached, axis=1, keepdims=True), jnp.max(fresh, axis=1, keepdims=True)
    )
    rate = HEAD_SIZE ** (-0.5) * math.log2(math.e)
    cached = jnp.exp2((cached - top) * rate)
    fresh = jnp.exp2((fresh - top) * rate)
    total = jnp.sum(cached, axis=1, keepdims=True) + jnp.sum(fresh, axis=1, keepdims=True)
    mixed = jnp.dot(
        cached.astype(jnp.bfloat16), prompt_values, preferred_element_type=jnp.float32
    ) + jnp.dot(fresh.astype(jnp.bfloat16), values, preferred_element_type=jnp.float32)
    live = lax.broadcasted_iota(jnp.int32, mixed.shape, 0) % span < length
    mixed = jnp.where(live, mixed / total, 0.0).astype(jnp.bfloat16)
    for h in range(heads):
        out_ref[0, :, h * HEAD_SIZE : (h + 1) * HEAD_SIZE] = mixed[h * span : (h + 1) * span]


def attention(span, q_width, projected, cache, keep_flag, destination, row_counts):
    cosine, sine = rope_tables(span, PROMPT_TOKENS)
    cosine = jnp.concatenate([cosine, cosine], axis=1)
    sine = jnp.concatenate([-sine, sine], axis=1)
    heads = q_width // HEAD_SIZE
    smem = pl.BlockSpec(memory_space=pltpu.SMEM)
    table = pl.BlockSpec((span, HEAD_SIZE), lambda s, p: (0, 0))
    return pl.pallas_call(
        attention_kernel,
        grid=(OUT_DEV, heads // 2),
        out_shape=jax.ShapeDtypeStruct((OUT_DEV, span, q_width), jnp.bfloat16),
        in_specs=[
            smem,
            smem,
            smem,
            table,
            table,
            pl.BlockSpec((span, 2 * HEAD_SIZE), lambda s, p: (s, p)),
            pl.BlockSpec((span, HEAD_SIZE), lambda s, p: (s, heads)),
            pl.BlockSpec((span, HEAD_SIZE), lambda s, p: (s, heads + 1)),
            pl.BlockSpec(cache.shape, lambda s, p: (0, 0, 0, 0)),
        ],
        out_specs=pl.BlockSpec((1, span, 2 * HEAD_SIZE), lambda s, p: (s, 0, p)),
        compiler_params=pltpu.CompilerParams(vmem_limit_bytes=48 * 1024 * 1024),
        name="attend",
    )(
        keep_flag,
        destination,
        row_counts,
        cosine,
        sine,
        projected,
        projected,
        projected,
        cache,
    )


def body(
    groups,
    shards,
    hidden,
    norm_gain,
    w_query,
    key_projection_weight,
    value_projection_weight,
    prompt_key_cache,
    prompt_value_cache,
    keep_flag,
    destination,
    row_counts,
):
    projected, cache = project(
        shards,
        groups,
        hidden,
        norm_gain,
        w_query,
        key_projection_weight,
        value_projection_weight,
        prompt_key_cache,
        prompt_value_cache,
        keep_flag,
        destination,
    )
    return attention(
        hidden.shape[1], w_query.shape[1], projected, cache, keep_flag, destination, row_counts
    )


def solution(mesh):
    return jax.shard_map(
        functools.partial(body, mesh.shape["group"], mesh.shape["fsdp"]),
        mesh=mesh,
        in_specs=(
            P("group", None, "fsdp"),
            P(),
            P("group", "fsdp"),
            P("group", None),
            P("group", None),
            P("group", None),
            P("group", None),
            P(),
            P(),
            P(),
        ),
        out_specs=P("group", None, "fsdp"),
        check_vma=False,
    )
```

time: 415 us -> 197 us (0.47)
  waiting for transfers between devices: 246 us -> 0 us
  Pallas kernels: 0 us -> 191 us
  matrix products: 58.2 us -> 0 us
  local copies, waits for them, and re-layouts: 34.2 us -> 4.32 us
  between operations: 28.5 us -> 0.08 us
  other arithmetic: 28.1 us -> 0.43 us
  blocking collectives: 14.2 us -> 0 us
  starting transfers between devices: 4.33 us -> 0 us
    all_gather x4 -> x0, waiting for transfers between devices: 240 us -> none  [the longest x1 105 us: attend(): gathered = lax.all_gather(blocks, 'fsdp', axis=2, tiled=True)]
    pallas_call x0 -> x2, Pallas kernels: none -> 191 us  [the longest x1 165 us: project(): pl.pallas_call(functools.partial(project_kernel, (groups, shards, lines,...]
    dot_general x7 -> x0, matrix products: 58.2 us -> none  [the longest x1 13.4 us: attend(): jnp.einsum('rhk,kd->rhd', powers.astype(jnp.bfloat16), pieces[1], preferr...]
    reduce_sum x3 -> x0, other arithmetic: 21.2 us -> none  [the longest x1 14.1 us: attend(): row_sum = jnp.sum(powers, axis=2)]
    dot_general x1 -> x0, local copies, waits for them, and re-layouts: 20.7 us -> none  [attend(): jnp.dot(normalized_input, pieces[0], preferred_element_type=jnp.float32)]
    all_gather x2 -> x0, blocking collectives: 14.2 us -> none  [the longest x1 7.28 us: attend(): lax.all_gather(prompt_keys, 'group', axis=0, tiled=True)]
    all_to_all x1 -> x0, waiting for transfers between devices: 5.43 us -> none  [body(): lax.all_to_all(packed, 'group', split_axis=0, concat_axis=0, tiled=True)]
    dynamic_slice x6 -> x0, local copies, waits for them, and re-layouts: 5.27 us -> none  [the longest x1 1.88 us: attend(): lax.dynamic_slice_in_dim(value_projection_weight, key_value_index * HEAD_...]
  transfers between devices with their start and end apart: 5 -> 0, of which waited for: 5 -> 0; matrix products, arithmetic and copies ran while one was open for 6% -> 0% of each run, Pallas kernels for 0% -> 0%
where the time goes in v2:
time: 197 us; the launch traced here: 196 us
  Pallas kernels  191 us (97%)
  local copies, waits for them, and re-layouts  4.32 us (2%)
    pallas_call x1, Pallas kernels, project(): pl.pallas_call(functools.partial(project_kernel, (groups, shards, lines,...  165 us
    pallas_call x1, Pallas kernels, attention(): pl.pallas_call(attention_kernel, grid=(OUT_DEV, heads // 2), out_shape=ja...  26.2 us

profile of v2, /device:TPU:0, one launch (start us, length us, event | category | flops | bytes accessed | tf_op | source)
XLA Modules:
  0.0 196.1 jit_solution(16489503033035658652)
XLA Ops:
  0.0 1.3 reshape.27.gain_ref
  1.4 0.3 fusion
  1.7 0.1 pad_maximum_fusion
  1.8 0.0 copy-start.2
  1.8 0.0 copy-start.3
  1.8 0.0 copy-start.4
  1.8 165.1 %gather_and_project.1 = (f32[512,1280]{1,0:T(8,128)}, bf16[4,2,512,128]{3,2,1,0:T(8,128)(2,1)}) custom-call(s32[32]{0:T(128)} %keep_ref.3, s32[32]{0:T(128)} %dest_ref.3, bf16[8,128,1024]{2,1,0:T(8,128)(2,1)} %hidden_ref.1, f32[8,1024]{1,0:T(8,128)} %reshape.27.gain_ref, bf16[2048,1024]{1,0:T(8,128)(2,1)} %wq_ref.1, bf16[2048,1024]{1,0:T(8,128)(2,1)} %wk_ref.1, ...), custom_call_target="tpu_custom_call" | custom-call | flops 10737418240 | bytes 5242880 | tf_op jit(solution)/shard_map/gather_and_project/pallas_call | solution.py:352
  166.9 0.0 copy-done.2
  166.9 0.0 copy-done.3
  167.0 0.0 copy-done.4
  167.0 0.0 copy-start
  167.0 1.7 copy-done
  168.7 0.0 copy-start.1
  168.7 1.2 copy-done.1
  169.9 26.2 %attend.1 = bf16[4,128,1024]{2,1,0:T(8,128)(2,1)} custom-call(s32[32]{0:T(128)S(1)} %copy-done.2, s32[32]{0:T(128)S(1)} %copy-done.3, s32[32]{0:T(128)S(1)} %copy-done.4, f32[128,128]{1,0:T(8,128)S(1)} %get-tuple-element.12.cos_ref, f32[128,128]{1,0:T(8,128)S(1)} %get-tuple-element.13.sin_ref, f32[512,1280]{1,0:T(8,128)S(1)} %copy-done, ...), custom_call_target="tpu_custom_call" | custom-call | tf_op jit(solution)/shard_map/attend/pallas_call | solution.py:451
  (2 shorter events, 0.0 us)
Async XLA Ops:
  1.8 165.1 %copy-start.2 = (s32[32]{0:T(128)S(1)}, s32[32]{0:T(128)}, u32[]{:S(2)}) copy-start(s32[32]{0:T(128)} %keep_ref.3) | copy-start | bytes 388
  1.8 165.1 %copy-start.3 = (s32[32]{0:T(128)S(1)}, s32[32]{0:T(128)}, u32[]{:S(2)}) copy-start(s32[32]{0:T(128)} %dest_ref.3) | copy-start | bytes 388
  1.8 165.1 %copy-start.4 = (s32[32]{0:T(128)S(1)}, s32[32]{0:T(128)}, u32[]{:S(2)}) copy-start(s32[32]{0:T(128)} %counts_ref.1) | copy-start | bytes 388
  167.0 1.7 copy-start
  168.7 1.2 copy-start.1

commit v3 on v2

--- a/solution.py
+++ b/solution.py
@@ -35,31 +35,35 @@
     return (jnp.cos(angles), jnp.sin(angles))
 
 
-CHUNKS = 4
 ROW_TILE = 16
-COLUMN_TILE = 2 * HEAD_SIZE
+PAIR = 2 * HEAD_SIZE
+GEMM_ROWS = 256
 MESH = pl.DeviceIdType.MESH
 
 
-def project_kernel(
+def sublayer_kernel(
     shape,
     keep_ref,
     dest_ref,
+    counts_ref,
     hidden_ref,
     gain_ref,
+    cos_ref,
+    sin_ref,
     wq_ref,
     wk_ref,
     wv_ref,
     kc_ref,
     vc_ref,
-    acc_ref,
-    cache_out_ref,
+    out_ref,
     outbox,
     inbox,
     x_all,
     x_norm,
-    w_all,
     cache,
+    q_rows,
+    new_keys,
+    new_values,
     local_sem,
     inbox_send,
     inbox_recv,
@@ -67,6 +71,7 @@
     x_recv,
     w_send,
     w_recv,
+    *w_all,
 ):
     groups, shards, lines, width = shape
     columns = shards // lines
@@ -74,7 +79,8 @@
     features = hidden_ref.shape[2]
     span = hidden_ref.shape[1]
     depth = wq_ref.shape[0]
-    chunk = depth // CHUNKS
+    pairs = wq_ref.shape[1] // PAIR
+    cached_chunk = pairs + 1
     heads = wq_ref.shape[1] // HEAD_SIZE
     group = lax.axis_index("group")
     shard = lax.axis_index("fsdp")
@@ -83,25 +89,29 @@
     head = shard * heads // (QUERY_HEADS // KEY_VALUE_HEADS)
     head_cols = pl.ds(pl.multiple_of(head * HEAD_SIZE, HEAD_SIZE), HEAD_SIZE)
 
-    local = []
-    for c in range(CHUNKS):
-        rows = pl.ds(c * chunk, chunk)
-        mine = w_all.at[group, c]
-        copies = [
+    local = [
+        [
             pltpu.make_async_copy(
-                wq_ref.at[rows, pl.ds(n * HEAD_SIZE, HEAD_SIZE)], mine.at[n], local_sem.at[c, n]
-            )
-            for n in range(heads)
+                ref.at[:, head_cols], w_all[0].at[group, n], local_sem.at[0, n]
+            )
+            for n, ref in enumerate((wk_ref, wv_ref))
         ]
-        for n, ref in ((heads, wk_ref), (heads + 1, wv_ref)):
-            copies.append(
-                pltpu.make_async_copy(ref.at[rows, head_cols], mine.at[n], local_sem.at[c, n])
-            )
-        local.append(copies)
+    ]
+    for c in range(pairs):
+        local.append(
+            [
+                pltpu.make_async_copy(
+                    wq_ref.at[:, pl.ds((2 * c + n) * HEAD_SIZE, HEAD_SIZE)],
+                    w_all[c + 1].at[group, n],
+                    local_sem.at[c + 1, n],
+                )
+                for n in range(2)
+            ]
+        )
     local.append(
         [
             pltpu.make_async_copy(
-                ref.at[:, head_cols], cache.at[group, n], local_sem.at[CHUNKS, n]
+                ref.at[:, head_cols], cache.at[group, n], local_sem.at[cached_chunk, n]
             )
             for n, ref in enumerate((kc_ref, vc_ref))
         ]
@@ -181,7 +191,7 @@
         )
 
     def w_copy(unit, c, hop):
-        ref = cache.at[unit] if c == CHUNKS else w_all.at[unit, c]
+        ref = (cache if c == cached_chunk else w_all[c]).at[unit]
         return pltpu.make_async_remote_copy(
             src_ref=ref,
             dst_ref=ref,
@@ -199,7 +209,7 @@
         sends.append((copy, when))
 
     always = group >= 0
-    order = [CHUNKS] + list(range(CHUNKS))
+    order = [cached_chunk] + list(range(pairs + 1))
     for c in order:
         for copy in local[c]:
             copy.wait()
@@ -273,7 +283,7 @@
                 launch(w_copy(unit, c, hop), there & w_hops[hop][0])
             launch(w_copy(unit, c, 2), there)
 
-    w_events = [(step, c) for step in range(1, chips) for c in order]
+    w_events = [(step, c) for c in order for step in range(1, chips)]
     w_chip(*w_events.pop(0))
     for step in range(1, columns):
         x_column(step)
@@ -296,36 +306,103 @@
         return carry
 
     lax.fori_loop(0, OUT_DEV * span // ROW_TILE, normalize, 0)
-    acc_ref[...] = jnp.zeros_like(acc_ref)
-
-    def multiply(unit, c):
-        block = unit * (depth // features) + c * chunk // features
-        inner = pl.ds(c * chunk % features, chunk)
-
-        def tile(n, carry):
-            cols = pl.ds(pl.multiple_of(n * COLUMN_TILE, COLUMN_TILE), COLUMN_TILE)
-            acc_ref[:, cols] += jnp.dot(
-                x_norm[block, :, inner],
-                jnp.concatenate([w_all[unit, c, 2 * n], w_all[unit, c, 2 * n + 1]], axis=1),
-                preferred_element_type=jnp.float32,
-            )
+
+    def arrive(position):
+        last = order[min(position, len(order) - 1)]
+        while any(c == last for _, c in w_events):
+            w_chip(*w_events.pop(0))
+
+    def from_partner(c):
+        for d in range(chips):
+            w_copy((chip + d) % chips * 2 + 1 - core, c, 2).wait_recv()
+
+    def multiply(c):
+        def tile(m, carry):
+            rows = pl.ds(pl.multiple_of(m * GEMM_ROWS, GEMM_ROWS), GEMM_ROWS)
+            total = jnp.zeros((GEMM_ROWS, PAIR), jnp.float32)
+            for f in range(shards):
+                unit = f * features // depth
+                inner = pl.ds(f * features % depth, features)
+                both = jnp.concatenate(
+                    [w_all[c][unit, 0, inner, :], w_all[c][unit, 1, inner, :]], axis=1
+                )
+                total = total + jnp.dot(
+                    x_norm[f, rows, :], both, preferred_element_type=jnp.float32
+                )
+            q_rows[rows, :] = total
             return carry
 
-        lax.fori_loop(0, acc_ref.shape[1] // COLUMN_TILE, tile, 0)
-
-    def from_partner(unit, c):
-        w_copy(unit, c, 2).wait_recv()
-
-    while w_events:
-        w_chip(*w_events.pop(0))
-    for d in range(chips):
-        for c in order:
-            from_partner((chip + d) % chips * 2 + 1 - core, c)
-    for unit in range(groups):
-        for c in range(CHUNKS):
-            multiply(unit, c)
-    result = pltpu.make_async_copy(cache, cache_out_ref, local_sem.at[CHUNKS, 2])
-    result.start()
+        lax.fori_loop(0, OUT_DEV * span // GEMM_ROWS, tile, 0)
+
+    def turn(values):
+        return (
+            values * cos_ref[...] + pltpu.roll(values, HEAD_SIZE // 2, 1) * sin_ref[...]
+        ).astype(jnp.bfloat16)
+
+    def keep_fresh(s, carry):
+        rows = pl.ds(pl.multiple_of(s * span, span), span)
+        new_keys[rows, :] = turn(q_rows[rows, pl.ds(0, HEAD_SIZE)])
+        new_values[rows, :] = q_rows[rows, pl.ds(HEAD_SIZE, HEAD_SIZE)].astype(jnp.bfloat16)
+        return carry
+
+    contract = (((1,), (1,)), ((), ()))
+    rate = HEAD_SIZE ** (-0.5) * math.log2(math.e)
+
+    def attend(pair):
+        def one_slot(s, carry):
+            slot = group * OUT_DEV + s
+
+            def find(b, length):
+                hit = (keep_ref[b] == 1) & (dest_ref[b] == slot)
+                return jnp.where(hit, counts_ref[b], length)
+
+            length = lax.fori_loop(0, groups * IN_DEV, find, jnp.int32(0))
+            rows = pl.ds(pl.multiple_of(s * span, span), span)
+            queries = jnp.concatenate(
+                [turn(q_rows[rows, pl.ds(h * HEAD_SIZE, HEAD_SIZE)]) for h in range(2)], axis=0
+            )
+            tokens = groups * cache.shape[2]
+            prompt_keys = cache[:, 0].reshape(tokens, HEAD_SIZE)
+            prompt_values = cache[:, 1].reshape(tokens, HEAD_SIZE)
+            cached = lax.dot_general(
+                queries, prompt_keys, contract, preferred_element_type=jnp.float32
+            )
+            fresh = lax.dot_general(
+                queries, new_keys[rows, :], contract, preferred_element_type=jnp.float32
+            )
+            row = lax.broadcasted_iota(jnp.int32, fresh.shape, 0) % span
+            column = lax.broadcasted_iota(jnp.int32, fresh.shape, 1)
+            fresh = jnp.where((column <= row) & (column < length), fresh, MASKED_SCORE)
+            top = jnp.maximum(
+                jnp.max(cached, axis=1, keepdims=True), jnp.max(fresh, axis=1, keepdims=True)
+            )
+            cached = jnp.exp2((cached - top) * rate)
+            fresh = jnp.exp2((fresh - top) * rate)
+            total = jnp.sum(cached, axis=1, keepdims=True) + jnp.sum(fresh, axis=1, keepdims=True)
+            mixed = jnp.dot(
+                cached.astype(jnp.bfloat16), prompt_values, preferred_element_type=jnp.float32
+            ) + jnp.dot(
+                fresh.astype(jnp.bfloat16), new_values[rows, :], preferred_element_type=jnp.float32
+            )
+            live = lax.broadcasted_iota(jnp.int32, mixed.shape, 0) % span < length
+            mixed = jnp.where(live, mixed / total, 0.0).astype(jnp.bfloat16)
+            for h in range(2):
+                columns_out = pl.ds(pair * PAIR + h * HEAD_SIZE, HEAD_SIZE)
+                out_ref[s, :, columns_out] = mixed[h * span : (h + 1) * span]
+            return carry
+
+        lax.fori_loop(0, OUT_DEV, one_slot, 0)
+
+    arrive(0)
+    from_partner(cached_chunk)
+    for c in range(pairs + 1):
+        arrive(c + 2)
+        from_partner(c)
+        multiply(c)
+        if c == 0:
+            lax.fori_loop(0, OUT_DEV, keep_fresh, 0)
+        else:
+            attend(c - 1)
     for post in posts:
         post.wait_send()
     for copy, when in sends:
@@ -334,148 +411,67 @@
         def _(copy=copy):
             copy.wait_send()
 
-    result.wait()
-
-
-def project(shards, groups, hidden, norm_gain, w_query, wk, wv, kc, vc, keep_flag, destination):
+
+def sublayer(
+    shards, groups, hidden, norm_gain, w_query, wk, wv, kc, vc, keep_flag, destination, row_counts
+):
     blocks, span, features = hidden.shape
     depth, q_width = w_query.shape
     width = norm_gain.shape[0]
     lines = math.isqrt(shards // 2)
     rows = OUT_DEV * span
-    out_width = q_width + 2 * HEAD_SIZE
+    pairs = q_width // PAIR
     cached = kc.shape[0]
+    cosine, sine = rope_tables(span, PROMPT_TOKENS)
     smem = pl.BlockSpec(memory_space=pltpu.SMEM)
     vmem = pl.BlockSpec(memory_space=pltpu.VMEM)
     anywhere = pl.BlockSpec(memory_space=pl.ANY)
     dma = pltpu.SemaphoreType.DMA
     return pl.pallas_call(
-        functools.partial(project_kernel, (groups, shards, lines, width)),
-        out_shape=(
-            jax.ShapeDtypeStruct((rows, out_width), jnp.float32),
-            jax.ShapeDtypeStruct((groups, 2, cached, HEAD_SIZE), jnp.bfloat16),
-        ),
-        in_specs=[smem, smem, vmem, vmem] + [anywhere] * 5,
-        out_specs=(vmem, anywhere),
+        functools.partial(sublayer_kernel, (groups, shards, lines, width)),
+        out_shape=jax.ShapeDtypeStruct((OUT_DEV, span, q_width), jnp.bfloat16),
+        in_specs=[smem] * 3 + [vmem] * 4 + [anywhere] * 5,
+        out_specs=vmem,
         scratch_shapes=[
             pltpu.VMEM((groups - 1, span, features), jnp.bfloat16),
             pltpu.VMEM((groups, span, features), jnp.bfloat16),
             pltpu.VMEM((shards, rows, features), jnp.bfloat16),
             pltpu.VMEM((shards, rows, features), jnp.bfloat16),
-            pltpu.VMEM((groups, CHUNKS, out_width // HEAD_SIZE, depth // CHUNKS, HEAD_SIZE), jnp.bfloat16),
             pltpu.VMEM((groups, 2, cached, HEAD_SIZE), jnp.bfloat16),
-            dma((CHUNKS + 1, out_width // HEAD_SIZE)),
+            pltpu.VMEM((rows, PAIR), jnp.float32),
+            pltpu.VMEM((rows, HEAD_SIZE), jnp.bfloat16),
+            pltpu.VMEM((rows, HEAD_SIZE), jnp.bfloat16),
+            dma((pairs + 2, 2)),
             dma((groups - 1,)),
             dma((groups,)),
             dma((shards, 4)),
             dma((shards,)),
-            dma((groups, CHUNKS + 1, 3)),
-            dma((groups, CHUNKS + 1)),
-        ],
+            dma((groups, pairs + 2, 3)),
+            dma((groups, pairs + 2)),
+        ]
+        + [pltpu.VMEM((groups, 2, depth, HEAD_SIZE), jnp.bfloat16)] * (pairs + 1),
         compiler_params=pltpu.CompilerParams(
-            collective_id=0, has_side_effects=True, vmem_limit_bytes=58 * 1024 * 1024
+            collective_id=0, has_side_effects=True, vmem_limit_bytes=60 * 1024 * 1024
         ),
         cost_estimate=pl.CostEstimate(
-            flops=2 * rows * width * out_width, bytes_accessed=depth * out_width * 2, transcendentals=0
+            flops=2 * rows * width * (q_width + PAIR),
+            bytes_accessed=depth * (q_width + PAIR) * 2,
+            transcendentals=0,
         ),
-        name="gather_and_project",
+        name="gather_project_attend",
     )(
         keep_flag,
         destination,
+        row_counts,
         hidden,
         norm_gain.astype(jnp.float32).reshape(shards, features),
+        jnp.concatenate([cosine, cosine], axis=1),
+        jnp.concatenate([-sine, sine], axis=1),
         w_query,
         wk,
         wv,
         kc,
         vc,
-    )
-
-
-def attention_kernel(
-    keep_ref, dest_ref, counts_ref, cos_ref, sin_ref, q_ref, k_ref, v_ref, cache_ref, out_ref
-):
-    slot = lax.axis_index("group") * OUT_DEV + pl.program_id(0)
-
-    def find(b, length):
-        hit = (keep_ref[b] == 1) & (dest_ref[b] == slot)
-        return jnp.where(hit, counts_ref[b], length)
-
-    length = lax.fori_loop(0, keep_ref.shape[0], find, jnp.int32(0))
-    cosine, sine = cos_ref[...], sin_ref[...]
-
-    def turn(values):
-        return (values * cosine + pltpu.roll(values, HEAD_SIZE // 2, 1) * sine).astype(jnp.bfloat16)
-
-    span = q_ref.shape[0]
-    heads = q_ref.shape[1] // HEAD_SIZE
-    queries = jnp.concatenate(
-        [turn(q_ref[:, h * HEAD_SIZE : (h + 1) * HEAD_SIZE]) for h in range(heads)], axis=0
-    )
-    keys = turn(k_ref[...])
-    values = v_ref[...].astype(jnp.bfloat16)
-    contract = (((1,), (1,)), ((), ()))
-    tokens = cache_ref.shape[0] * cache_ref.shape[2]
-    prompt_keys = cache_ref[:, 0].reshape(tokens, HEAD_SIZE)
-    prompt_values = cache_ref[:, 1].reshape(tokens, HEAD_SIZE)
-    cached = lax.dot_general(
-        queries, prompt_keys, contract, preferred_element_type=jnp.float32
-    )
-    fresh = lax.dot_general(queries, keys, contract, preferred_element_type=jnp.float32)
-    row = lax.broadcasted_iota(jnp.int32, fresh.shape, 0) % span
-    column = lax.broadcasted_iota(jnp.int32, fresh.shape, 1)
-    fresh = jnp.where((column <= row) & (column < length), fresh, MASKED_SCORE)
-    top = jnp.maximum(
-        jnp.max(cached, axis=1, keepdims=True), jnp.max(fresh, axis=1, keepdims=True)
-    )
-    rate = HEAD_SIZE ** (-0.5) * math.log2(math.e)
-    cached = jnp.exp2((cached - top) * rate)
-    fresh = jnp.exp2((fresh - top) * rate)
-    total = jnp.sum(cached, axis=1, keepdims=True) + jnp.sum(fresh, axis=1, keepdims=True)
-    mixed = jnp.dot(
-        cached.astype(jnp.bfloat16), prompt_values, preferred_element_type=jnp.float32
-    ) + jnp.dot(fresh.astype(jnp.bfloat16), values, preferred_element_type=jnp.float32)
-    live = lax.broadcasted_iota(jnp.int32, mixed.shape, 0) % span < length
-    mixed = jnp.where(live, mixed / total, 0.0).astype(jnp.bfloat16)
-    for h in range(heads):
-        out_ref[0, :, h * HEAD_SIZE : (h + 1) * HEAD_SIZE] = mixed[h * span : (h + 1) * span]
-
-
-def attention(span, q_width, projected, cache, keep_flag, destination, row_counts):
-    cosine, sine = rope_tables(span, PROMPT_TOKENS)
-    cosine = jnp.concatenate([cosine, cosine], axis=1)
-    sine = jnp.concatenate([-sine, sine], axis=1)
-    heads = q_width // HEAD_SIZE
-    smem = pl.BlockSpec(memory_space=pltpu.SMEM)
-    table = pl.BlockSpec((span, HEAD_SIZE), lambda s, p: (0, 0))
-    return pl.pallas_call(
-        attention_kernel,
-        grid=(OUT_DEV, heads // 2),
-        out_shape=jax.ShapeDtypeStruct((OUT_DEV, span, q_width), jnp.bfloat16),
-        in_specs=[
-            smem,
-            smem,
-            smem,
-            table,
-            table,
-            pl.BlockSpec((span, 2 * HEAD_SIZE), lambda s, p: (s, p)),
-            pl.BlockSpec((span, HEAD_SIZE), lambda s, p: (s, heads)),
-            pl.BlockSpec((span, HEAD_SIZE), lambda s, p: (s, heads + 1)),
-            pl.BlockSpec(cache.shape, lambda s, p: (0, 0, 0, 0)),
-        ],
-        out_specs=pl.BlockSpec((1, span, 2 * HEAD_SIZE), lambda s, p: (s, 0, p)),
-        compiler_params=pltpu.CompilerParams(vmem_limit_bytes=48 * 1024 * 1024),
-        name="attend",
-    )(
-        keep_flag,
-        destination,
-        row_counts,
-        cosine,
-        sine,
-        projected,
-        projected,
-        projected,
-        cache,
     )
 
 
@@ -493,7 +489,7 @@
     destination,
     row_counts,
 ):
-    projected, cache = project(
+    return sublayer(
         shards,
         groups,
         hidden,
@@ -505,9 +501,7 @@
         prompt_value_cache,
         keep_flag,
         destination,
-    )
-    return attention(
-        hidden.shape[1], w_query.shape[1], projected, cache, keep_flag, destination, row_counts
+        row_counts,
     )
 
 

time: 197 us -> 160 us (0.81)
  Pallas kernels: 191 us -> 155 us
    pallas_call x2 -> x1, Pallas kernels: 191 us -> 155 us  [sublayer(): pl.pallas_call(functools.partial(sublayer_kernel, (groups, shards, lines,...]
where the time goes in v3:
time: 160 us
  Pallas kernels  155 us (97%)
  local copies, waits for them, and re-layouts  3.6 us (2%)
    pallas_call x1, Pallas kernels, sublayer(): pl.pallas_call(functools.partial(sublayer_kernel, (groups, shards, lines,...  155 us

profile of v3, /device:TPU:0, one launch (start us, length us, event | category | flops | bytes accessed | tf_op | source)
XLA Modules:
  0.0 159.9 jit_solution(13886491017352427246)
XLA Ops:
  0.0 1.3 reshape.27.gain_ref
  1.4 0.3 fusion
  1.7 0.8 pad_maximum_fusion
  2.4 155.2 %gather_project_attend.1 = bf16[4,128,1024]{2,1,0:T(8,128)(2,1)} custom-call(s32[32]{0:T(128)} %keep_ref.1, s32[32]{0:T(128)} %dest_ref.1, s32[32]{0:T(128)} %counts_ref.1, bf16[8,128,1024]{2,1,0:T(8,128)(2,1)} %hidden_ref.1, f32[8,1024]{1,0:T(8,128)} %reshape.27.gain_ref, f32[128,128]{1,0:T(8,128)} %get-tuple-element.8.cos_ref, ...), custom_call_target="tpu_custom_call" | custom-call | flops 10737418240 | bytes 5242880 | tf_op jit(solution)/shard_map/gather_project_attend/pallas_call | solution.py:430
  157.7 2.3 %copy.12 = bf16[4,128,1024]{2,1,0:T(8,128)(2,1)} copy(bf16[4,128,1024]{2,1,0:T(8,128)(2,1)} %gather_project_attend.1) | data formatting | bytes 2097152
  (2 shorter events, 0.0 us)

commit v4 on v3

--- a/solution.py
+++ b/solution.py
@@ -37,7 +37,7 @@
 
 ROW_TILE = 16
 PAIR = 2 * HEAD_SIZE
-GEMM_ROWS = 256
+HALF_SLOTS = OUT_DEV // 2
 MESH = pl.DeviceIdType.MESH
 
 
@@ -58,7 +58,8 @@
     out_ref,
     outbox,
     inbox,
-    x_all,
+    x_first,
+    x_second,
     x_norm,
     cache,
     q_rows,
@@ -79,6 +80,8 @@
     features = hidden_ref.shape[2]
     span = hidden_ref.shape[1]
     depth = wq_ref.shape[0]
+    half_rows = HALF_SLOTS * span
+    x_all = (x_first, x_second)
     pairs = wq_ref.shape[1] // PAIR
     cached_chunk = pairs + 1
     heads = wq_ref.shape[1] // HEAD_SIZE
@@ -170,22 +173,22 @@
 
     sends = []
 
-    def x_copy(unit, hop):
+    def x_copy(half, unit, hop):
         return pltpu.make_async_remote_copy(
-            src_ref=x_all.at[unit],
-            dst_ref=x_all.at[unit],
-            send_sem=x_send.at[unit, hop],
-            recv_sem=x_recv.at[unit],
+            src_ref=x_all[half].at[unit],
+            dst_ref=x_all[half].at[unit],
+            send_sem=x_send.at[half, unit, hop],
+            recv_sem=x_recv.at[half, unit],
             device_id={"fsdp": x_hops[hop][1]},
             device_id_type=MESH,
         )
 
-    def x_arrival(unit):
+    def x_arrival(half, unit):
         return pltpu.make_async_remote_copy(
-            src_ref=x_all.at[unit],
-            dst_ref=x_all.at[unit],
-            send_sem=x_send.at[unit, 0],
-            recv_sem=x_recv.at[unit],
+            src_ref=x_all[half].at[unit],
+            dst_ref=x_all[half].at[unit],
+            send_sem=x_send.at[half, unit, 0],
+            recv_sem=x_recv.at[half, unit],
             device_id={"fsdp": (shard + 1) % shards},
             device_id_type=MESH,
         )
@@ -235,12 +238,13 @@
             return jnp.where(hit, lax.div(b, jnp.int32(IN_DEV)), owner)
 
         owner = lax.fori_loop(0, groups * IN_DEV, find, jnp.int32(0))
-        x_all[shard, pl.ds(o * span, span), :] = inbox[owner]
-
-    for hop in range(4):
-        launch(x_copy(shard, hop), x_hops[hop][0])
-
-    def x_column(step):
+        x_all[o // HALF_SLOTS][shard, pl.ds(o % HALF_SLOTS * span, span), :] = inbox[owner]
+
+    def x_own(half):
+        for hop in range(4):
+            launch(x_copy(half, shard, hop), x_hops[hop][0])
+
+    def x_column(step, half):
         for hop, sign in ((0, 1), (1, -1)):
             source = col - sign * step
             there = (source >= 0) & (source < columns)
@@ -248,14 +252,14 @@
 
             @pl.when(there)
             def _(unit=unit):
-                x_arrival(unit).wait_recv()
+                x_arrival(half, unit).wait_recv()
 
             if step < columns - 1:
-                launch(x_copy(unit, hop), there & x_hops[hop][0])
+                launch(x_copy(half, unit, hop), there & x_hops[hop][0])
             for side in (2, 3):
-                launch(x_copy(unit, side), there & x_hops[side][0])
-
-    def x_line(step):
+                launch(x_copy(half, unit, side), there & x_hops[side][0])
+
+    def x_line(step, half):
         for hop, sign in ((2, 1), (3, -1)):
             source = line - sign * step
             there = (source >= 0) & (source < lines)
@@ -264,10 +268,10 @@
 
                 @pl.when(there)
                 def _(unit=unit):
-                    x_arrival(unit).wait_recv()
+                    x_arrival(half, unit).wait_recv()
 
                 if step < lines - 1:
-                    launch(x_copy(unit, hop), there & x_hops[hop][0])
+                    launch(x_copy(half, unit, hop), there & x_hops[hop][0])
 
     def w_chip(step, c):
         for hop, sign in ((0, 1), (1, -1)):
@@ -284,31 +288,27 @@
             launch(w_copy(unit, c, 2), there)
 
     w_events = [(step, c) for c in order for step in range(1, chips)]
-    w_chip(*w_events.pop(0))
-    for step in range(1, columns):
-        x_column(step)
-        if len(w_events) > 2:
-            w_chip(*w_events.pop(0))
-    for step in range(1, lines):
-        x_line(step)
-
-    def normalize(i, carry):
-        rows = pl.ds(pl.multiple_of(i * ROW_TILE, ROW_TILE), ROW_TILE)
-        total = jnp.zeros((ROW_TILE, features), jnp.float32)
-        for f in range(shards):
-            values = x_all[f, rows, :].astype(jnp.float32)
-            total = total + values * values
-        mean = jnp.sum(total, axis=1, keepdims=True) / width
-        factor = lax.rsqrt(mean + EPSILON)
-        for f in range(shards):
-            values = x_all[f, rows, :].astype(jnp.float32)
-            x_norm[f, rows, :] = (values * factor * gain_ref[pl.ds(f, 1), :]).astype(jnp.bfloat16)
-        return carry
-
-    lax.fori_loop(0, OUT_DEV * span // ROW_TILE, normalize, 0)
-
-    def arrive(position):
-        last = order[min(position, len(order) - 1)]
+    def normalize(half):
+        def tile(i, carry):
+            start = pl.multiple_of(i * ROW_TILE, ROW_TILE)
+            rows = pl.ds(start, ROW_TILE)
+            rows_out = pl.ds(half * half_rows + start, ROW_TILE)
+            total = jnp.zeros((ROW_TILE, features), jnp.float32)
+            for f in range(shards):
+                values = x_all[half][f, rows, :].astype(jnp.float32)
+                total = total + values * values
+            mean = jnp.sum(total, axis=1, keepdims=True) / width
+            factor = lax.rsqrt(mean + EPSILON)
+            for f in range(shards):
+                values = x_all[half][f, rows, :].astype(jnp.float32)
+                x_norm[f, rows_out, :] = (values * factor * gain_ref[pl.ds(f, 1), :]).astype(
+                    jnp.bfloat16
+                )
+            return carry
+
+        lax.fori_loop(0, half_rows // ROW_TILE, tile, 0)
+
+    def arrive(last):
         while any(c == last for _, c in w_events):
             w_chip(*w_events.pop(0))
 
@@ -316,23 +316,17 @@
         for d in range(chips):
             w_copy((chip + d) % chips * 2 + 1 - core, c, 2).wait_recv()
 
-    def multiply(c):
-        def tile(m, carry):
-            rows = pl.ds(pl.multiple_of(m * GEMM_ROWS, GEMM_ROWS), GEMM_ROWS)
-            total = jnp.zeros((GEMM_ROWS, PAIR), jnp.float32)
-            for f in range(shards):
-                unit = f * features // depth
-                inner = pl.ds(f * features % depth, features)
-                both = jnp.concatenate(
-                    [w_all[c][unit, 0, inner, :], w_all[c][unit, 1, inner, :]], axis=1
-                )
-                total = total + jnp.dot(
-                    x_norm[f, rows, :], both, preferred_element_type=jnp.float32
-                )
-            q_rows[rows, :] = total
-            return carry
-
-        lax.fori_loop(0, OUT_DEV * span // GEMM_ROWS, tile, 0)
+    def multiply(c, half):
+        rows = pl.ds(half * half_rows, half_rows)
+        total = jnp.zeros((half_rows, PAIR), jnp.float32)
+        for f in range(shards):
+            unit = f * features // depth
+            inner = pl.ds(f * features % depth, features)
+            both = jnp.concatenate(
+                [w_all[c][unit, 0, inner, :], w_all[c][unit, 1, inner, :]], axis=1
+            )
+            total = total + jnp.dot(x_norm[f, rows, :], both, preferred_element_type=jnp.float32)
+        q_rows[rows, :] = total
 
     def turn(values):
         return (
@@ -348,7 +342,7 @@
     contract = (((1,), (1,)), ((), ()))
     rate = HEAD_SIZE ** (-0.5) * math.log2(math.e)
 
-    def attend(pair):
+    def attend(pair, half):
         def one_slot(s, carry):
             slot = group * OUT_DEV + s
 
@@ -391,18 +385,52 @@
                 out_ref[s, :, columns_out] = mixed[h * span : (h + 1) * span]
             return carry
 
-        lax.fori_loop(0, OUT_DEV, one_slot, 0)
-
+        lax.fori_loop(half * HALF_SLOTS, (half + 1) * HALF_SLOTS, one_slot, 0)
+
+    def keys_and_values(half):
+        multiply(0, half)
+        lax.fori_loop(half * HALF_SLOTS, (half + 1) * HALF_SLOTS, keep_fresh, 0)
+
+    def heads_of(c, half):
+        multiply(c, half)
+        attend(c - 1, half)
+
+    x_own(0)
+    arrive(cached_chunk)
+    for step in range(1, columns):
+        x_column(step, 0)
+        if step == columns - 2:
+            arrive(0)
     arrive(0)
+    x_own(1)
+    x_column(1, 1)
+    for step in range(1, lines):
+        x_line(step, 0)
+    normalize(0)
     from_partner(cached_chunk)
-    for c in range(pairs + 1):
-        arrive(c + 2)
+    from_partner(0)
+    keys_and_values(0)
+    ahead = 0
+    for step in range(2, columns):
+        x_column(step, 1)
+        if ahead < pairs - 2:
+            ahead += 1
+            arrive(ahead)
+            from_partner(ahead)
+            heads_of(ahead, 0)
+    for step in range(1, lines):
+        x_line(step, 1)
+    normalize(1)
+    keys_and_values(1)
+    arrive(ahead + 1)
+    for c in range(1, ahead + 1):
+        heads_of(c, 1)
+    for c in range(ahead + 1, pairs + 1):
         from_partner(c)
-        multiply(c)
-        if c == 0:
-            lax.fori_loop(0, OUT_DEV, keep_fresh, 0)
-        else:
-            attend(c - 1)
+        heads_of(c, 0)
+        if c < pairs:
+            arrive(c + 1)
+        heads_of(c, 1)
     for post in posts:
         post.wait_send()
     for copy, when in sends:
@@ -435,7 +463,8 @@
         scratch_shapes=[
             pltpu.VMEM((groups - 1, span, features), jnp.bfloat16),
             pltpu.VMEM((groups, span, features), jnp.bfloat16),
-            pltpu.VMEM((shards, rows, features), jnp.bfloat16),
+            pltpu.VMEM((shards, rows // 2, features), jnp.bfloat16),
+            pltpu.VMEM((shards, rows // 2, features), jnp.bfloat16),
             pltpu.VMEM((shards, rows, features), jnp.bfloat16),
             pltpu.VMEM((groups, 2, cached, HEAD_SIZE), jnp.bfloat16),
             pltpu.VMEM((rows, PAIR), jnp.float32),
@@ -444,8 +473,8 @@
             dma((pairs + 2, 2)),
             dma((groups - 1,)),
             dma((groups,)),
-            dma((shards, 4)),
-            dma((shards,)),
+            dma((2, shards, 4)),
+            dma((2, shards)),
             dma((groups, pairs + 2, 3)),
             dma((groups, pairs + 2)),
         ]

time: 160 us -> 156 us (0.975)
  Pallas kernels: 155 us -> 151 us
    pallas_call x1, Pallas kernels: 155 us -> 151 us  [sublayer(): pl.pallas_call(functools.partial(sublayer_kernel, (groups, shards, lines,...]
where the time goes in v4:
time: 156 us
  Pallas kernels  151 us (97%)
  local copies, waits for them, and re-layouts  3.6 us (2%)
    pallas_call x1, Pallas kernels, sublayer(): pl.pallas_call(functools.partial(sublayer_kernel, (groups, shards, lines,...  151 us

profile of v4, /device:TPU:0, one launch (start us, length us, event | category | flops | bytes accessed | tf_op | source)
XLA Modules:
  0.0 156.1 jit_solution(15184486633862413644)
XLA Ops:
  0.0 1.3 reshape.27.gain_ref
  1.4 0.3 fusion
  1.7 0.8 pad_maximum_fusion
  2.4 151.4 %gather_project_attend.1 = bf16[4,128,1024]{2,1,0:T(8,128)(2,1)} custom-call(s32[32]{0:T(128)} %keep_ref.1, s32[32]{0:T(128)} %dest_ref.1, s32[32]{0:T(128)} %counts_ref.1, bf16[8,128,1024]{2,1,0:T(8,128)(2,1)} %hidden_ref.1, f32[8,1024]{1,0:T(8,128)} %reshape.27.gain_ref, f32[128,128]{1,0:T(8,128)} %get-tuple-element.8.cos_ref, ...), custom_call_target="tpu_custom_call" | custom-call | flops 10737418240 | bytes 5242880 | tf_op jit(solution)/shard_map/gather_project_attend/pallas_call | solution.py:458
  153.8 2.3 %copy.12 = bf16[4,128,1024]{2,1,0:T(8,128)(2,1)} copy(bf16[4,128,1024]{2,1,0:T(8,128)(2,1)} %gather_project_attend.1) | data formatting | bytes 2097152
  (2 shorter events, 0.0 us)

commit v5 on v4

--- a/solution.py
+++ b/solution.py
@@ -213,12 +213,18 @@
 
     always = group >= 0
     order = [cached_chunk] + list(range(pairs + 1))
-    for c in order:
-        for copy in local[c]:
-            copy.wait()
-        for hop in (0, 1):
-            launch(w_copy(group, c, hop), w_hops[hop][0])
-        launch(w_copy(group, c, 2), always)
+
+    def w_own(position):
+        if position < len(order):
+            c = order[position]
+            for copy in local[c]:
+                copy.wait()
+            for hop in (0, 1):
+                launch(w_copy(group, c, hop), w_hops[hop][0])
+            launch(w_copy(group, c, 2), always)
+
+    w_own(0)
+    w_own(1)
 
     for j in range(1, groups):
         source = (group + j) % groups
@@ -286,6 +292,8 @@
             if step < chips - 1:
                 launch(w_copy(unit, c, hop), there & w_hops[hop][0])
             launch(w_copy(unit, c, 2), there)
+        if step == 1:
+            w_own(order.index(c) + 2)
 
     w_events = [(step, c) for c in order for step in range(1, chips)]
     def normalize(half):

time: 156 us -> 156 us (level)
  no operation moved by 1% of the time
where the time goes in v5:
time: 156 us
  Pallas kernels  151 us (97%)
  local copies, waits for them, and re-layouts  3.6 us (2%)
    pallas_call x1, Pallas kernels, sublayer(): pl.pallas_call(functools.partial(sublayer_kernel, (groups, shards, lines,...  151 us

profile of v5, /device:TPU:0, one launch (start us, length us, event | category | flops | bytes accessed | tf_op | source)
XLA Modules:
  0.0 156.1 jit_solution(6165848336621586339)
XLA Ops:
  0.0 1.3 reshape.27.gain_ref
  1.4 0.3 fusion
  1.7 0.8 pad_maximum_fusion
  2.4 151.4 %gather_project_attend.1 = bf16[4,128,1024]{2,1,0:T(8,128)(2,1)} custom-call(s32[32]{0:T(128)} %keep_ref.1, s32[32]{0:T(128)} %dest_ref.1, s32[32]{0:T(128)} %counts_ref.1, bf16[8,128,1024]{2,1,0:T(8,128)(2,1)} %hidden_ref.1, f32[8,1024]{1,0:T(8,128)} %reshape.27.gain_ref, f32[128,128]{1,0:T(8,128)} %get-tuple-element.8.cos_ref, ...), custom_call_target="tpu_custom_call" | custom-call | flops 10737418240 | bytes 5242880 | tf_op jit(solution)/shard_map/gather_project_attend/pallas_call | solution.py:466
  153.8 2.3 %copy.12 = bf16[4,128,1024]{2,1,0:T(8,128)(2,1)} copy(bf16[4,128,1024]{2,1,0:T(8,128)(2,1)} %gather_project_attend.1) | data formatting | bytes 2097152
  (2 shorter events, 0.0 us)
